TPU v7x, 512 devices: a whole 4x4x16 slice. The times are simulated.
512 devices in a mesh: gx: 32 (over z, core), gy: 16 (over y, x).
Axes of the slice: x: 4, y: 4, z: 16, core: 2. Of those that a mesh axis runs over, the one named last changes fastest.
Arguments:
- solution: float32 [512, 65536], P(None, ('gx', 'gy')), may hold values from -6 to 6
- residual: float32 [512, 65536], P(None, ('gx', 'gy')), may hold values from -60 to 60
- metric_diag: bfloat16 [3, 512, 65536], P(None, None, ('gx', 'gy')), may hold values from 0.039794922 to 0.3984375
- metric_cross: bfloat16 [3, 512, 65536], P(None, None, ('gx', 'gy')), may hold values from -0.017944336 to 0.017944336
- fdm_vectors: float32 [3, 8, 8, 65536], P(None, None, None, ('gx', 'gy')), may hold values from -5 to 5
- fdm_values: float32 [3, 8, 65536], P(None, None, ('gx', 'gy')), may hold values from 0.05 to 20
- vertex_ids: int32 [8, 65536], P(None, ('gx', 'gy')), may hold values from 0 to 8191
- coarse_inverse: float32 [8192, 8192], P(('gx', 'gy')), may hold values from -0.2 to 0.2, as said below
- elem_live: int32 [512], P(('gx', 'gy')), may hold values from 80 to 128, as said below
- section_face: int32 [512, 16, 20], P(('gx', 'gy')), may hold values from -1 to 767, as said below
- section_code: int32 [512, 16, 20], P(('gx', 'gy')), may hold values from 0 to 7, as said below
- pipe_face: int32 [512, 2, 64], P(('gx', 'gy')), may hold values from 0 to 767, as said below
- pipe_code: int32 [512, 2, 64], P(('gx', 'gy')), may hold values from 0 to 7, as said below
Outputs:
- solution_out: float32 [512, 65536], P(None, ('gx', 'gy'))
- residual_out: float32 [512, 65536], P(None, ('gx', 'gy'))
- norm_ratio: float32 [1], replicated
Inputs may be any that keep to these rules, and one draw needn't show every extreme that they name: `elem_live`: one device holds all 128 slots in every draw. A face id 6 e + f names face f of slot e of the device, with e below the device's elem_live; no id appears twice on a device over section_face and pipe_face; -1 marks an empty slot, and in each peer's row the slots holding faces come first. Slot (q, c) of device (x, y) holds a face exactly when slot (y, c) of device (x, q) does; in the row q = y they come in pairs (c, c xor 1). Each device's rows for peers y - 1, y + 1 and y + 16 / 2 (mod 16) are full; rows for other peers more than two places away (mod 16) are empty. `section_code`: with inv(o) = o for o < 4 and 4 + 2 (o mod 2) + floor((o mod 4) / 2) for o >= 4, the codes of two paired slots are inv of each other; empty slots hold 0. `pipe_face`: every slot holds a face, as for section_face. `pipe_code`: the codes of two paired slots are inv of each other, as for section_code. `coarse_inverse`: Symmetric.
All inputs are finite; a program needn't handle non-finite values.
Results may differ from a plain program's by a relative error of at most 0.0003.
Values sent between devices are 32-bit elements; how exact they have to be, the bound alone decides.
A program may use at most 64 MiB of HBM per device.

v0:
```python
import jax
import jax.numpy as jnp
from jax import lax
from jax.sharding import PartitionSpec as P

EDGE = 8


top_precision = lax.Precision.HIGHEST


def padded(block, sides, width):
    for axis, dim in sides:
        count = lax.axis_size(axis)
        forward = [(i, i + 1) for i in range(count - 1)]
        forward.append((count - 1, 0))
        backward = [(target, source) for source, target in forward]
        low = lax.ppermute(
            lax.slice_in_dim(block, block.shape[dim] - width, None, axis=dim), axis, forward
        )
        high = lax.ppermute(lax.slice_in_dim(block, 0, width, axis=dim), axis, backward)
        block = jnp.concatenate([low, block, high], axis=dim)
    return block


def node_points():
    node_index = jnp.arange(EDGE).astype(jnp.float32)
    return -jnp.cos(jnp.pi * node_index / (EDGE - 1))


def derivative_matrix():
    points = node_points()
    node_index = jnp.arange(EDGE)
    weights = jnp.where((node_index == 0) | (node_index == EDGE - 1), 2.0, 1.0).astype(jnp.float32)
    parity = jnp.where((node_index[:, None] + node_index[None, :]) % 2 == 0, 1.0, -1.0).astype(
        jnp.float32
    )
    identity = jnp.eye(EDGE, dtype=jnp.float32)
    spacing = points[:, None] - points[None, :] + identity
    offdiag = weights[:, None] / weights[None, :] * parity / spacing * (1.0 - identity)
    return offdiag - jnp.diag(jnp.sum(offdiag, axis=1))


def corner_table():
    points = node_points()
    hat_values = jnp.stack([(1.0 - points) * 0.5, (1.0 + points) * 0.5])
    corner_weights = (
        hat_values[:, None, None, :, None, None]
        * hat_values[None, :, None, None, :, None]
        * hat_values[None, None, :, None, None, :]
    )
    return corner_weights.reshape(8, EDGE**3)


def contract(matrices, element_cube, axis):
    moved = jnp.moveaxis(element_cube, axis, 0)
    total = matrices[0][:, None, None, :] * moved[0][None]
    for index in range(1, EDGE):
        total = total + matrices[index][:, None, None, :] * moved[index][None]
    return jnp.moveaxis(total, 0, axis)


def orient_columns(face_cols, orient_codes):
    face_grid = face_cols.reshape(EDGE, EDGE, -1)
    face_grid = jnp.where((orient_codes % 2 == 1)[None, None, :], face_grid[::-1, :, :], face_grid)
    face_grid = jnp.where(
        (orient_codes // 2 % 2 == 1)[None, None, :], face_grid[:, ::-1, :], face_grid
    )
    face_grid = jnp.where(
        (orient_codes >= 4)[None, None, :], jnp.swapaxes(face_grid, 0, 1), face_grid
    )
    return face_grid.reshape(EDGE * EDGE, -1)


def fdm_solve(element_cube, vectors, values):
    spectral = contract(vectors[0], element_cube, 0)
    spectral = contract(vectors[1], spectral, 1)
    spectral = contract(vectors[2], spectral, 2)
    eigen_sums = (
        values[0][:, None, None, :] + values[1][None, :, None, :] + values[2][None, None, :, :]
    )
    spectral = spectral / eigen_sums
    restored = contract(jnp.swapaxes(vectors[0], 0, 1), spectral, 0)
    restored = contract(jnp.swapaxes(vectors[1], 0, 1), restored, 1)
    return contract(jnp.swapaxes(vectors[2], 0, 1), restored, 2)


def local_operator(field, diag_part, cross_part, derivative):
    element_cube = field.reshape(EDGE, EDGE, EDGE, -1)
    diagonal = diag_part.astype(jnp.float32).reshape(3, EDGE, EDGE, EDGE, -1)
    cross_terms = cross_part.astype(jnp.float32).reshape(3, EDGE, EDGE, EDGE, -1)
    forward = jnp.transpose(derivative)[:, :, None]
    backward = derivative[:, :, None]
    grad_first = contract(forward, element_cube, 0)
    grad_second = contract(forward, element_cube, 1)
    grad_third = contract(forward, element_cube, 2)
    flux_first = (
        diagonal[0] * grad_first + cross_terms[0] * grad_second + cross_terms[1] * grad_third
    )
    flux_second = (
        cross_terms[0] * grad_first + diagonal[1] * grad_second + cross_terms[2] * grad_third
    )
    flux_third = (
        cross_terms[1] * grad_first + cross_terms[2] * grad_second + diagonal[2] * grad_third
    )
    curvature = jnp.sum(
        grad_first * flux_first + grad_second * flux_second + grad_third * flux_third
    ) + jnp.sum(element_cube * element_cube)
    applied = contract(backward, flux_first, 0)
    applied = applied + contract(backward, flux_second, 1)
    applied = applied + contract(backward, flux_third, 2)
    return ((applied + element_cube).reshape(EDGE**3, -1), curvature)


def face_sum(field, section_face, section_code, pipe_face, pipe_code):
    element_cube = field.reshape(EDGE, EDGE, EDGE, -1)
    slot_count = element_cube.shape[3]
    stacked = jnp.stack(
        [
            element_cube[0],
            element_cube[EDGE - 1],
            element_cube[:, 0],
            element_cube[:, EDGE - 1],
            element_cube[:, :, 0],
            element_cube[:, :, EDGE - 1],
        ],
        axis=-1,
    )
    face_values = stacked.reshape(EDGE * EDGE, slot_count * 6)
    face_count = face_values.shape[1]
    peer_count = section_face.shape[1]
    capacity = section_face.shape[2]
    wanted = section_face[0].reshape(-1)
    picked = jnp.take(face_values, jnp.maximum(wanted, 0), axis=1)
    outgoing = jnp.where((wanted >= 0)[None, :], picked, 0.0).reshape(
        EDGE * EDGE, peer_count, capacity
    )
    own_index = lax.axis_index("gy")
    arrived = lax.all_to_all(outgoing, "gy", split_axis=1, concat_axis=1, tiled=True)
    swapped = arrived.reshape(EDGE * EDGE, peer_count, capacity // 2, 2)[..., ::-1].reshape(
        EDGE * EDGE, peer_count, capacity
    )
    arrived = jnp.where((jnp.arange(peer_count) == own_index)[None, :, None], swapped, arrived)
    incoming = orient_columns(
        arrived.reshape(EDGE * EDGE, peer_count * capacity), section_code[0].reshape(-1)
    )
    pipe_ids = pipe_face[0]
    pipe_width = pipe_ids.shape[1]
    boundary = jnp.take(face_values, pipe_ids.reshape(-1), axis=1).reshape(
        EDGE * EDGE, 2, pipe_width
    )
    extended = padded(boundary, (("gx", 1),), 1)
    beside = jnp.concatenate([extended[:, 0], extended[:, 3]], axis=1)
    beside = orient_columns(beside, pipe_code[0].reshape(-1))
    targets = jnp.concatenate([wanted, pipe_ids.reshape(-1)])
    placed = jnp.where(targets < 0, face_count, targets)
    face_extra = (
        jnp.zeros((EDGE * EDGE, face_count), jnp.float32)
        .at[:, placed]
        .add(jnp.concatenate([incoming, beside], axis=1), mode="drop")
    )
    face_parts = face_extra.reshape(EDGE, EDGE, slot_count, 6)
    element_cube = element_cube.at[0].add(face_parts[..., 0])
    element_cube = element_cube.at[EDGE - 1].add(face_parts[..., 1])
    element_cube = element_cube.at[:, 0].add(face_parts[..., 2])
    element_cube = element_cube.at[:, EDGE - 1].add(face_parts[..., 3])
    element_cube = element_cube.at[:, :, 0].add(face_parts[..., 4])
    element_cube = element_cube.at[:, :, EDGE - 1].add(face_parts[..., 5])
    return element_cube.reshape(EDGE**3, -1)


def on_device(
    solution,
    residual,
    metric_diag,
    metric_cross,
    fdm_vectors,
    fdm_values,
    vertex_ids,
    coarse_inverse,
    elem_live,
    section_face,
    section_code,
    pipe_face,
    pipe_code,
):
    slot_count = residual.shape[1]
    alive_mask = (jnp.arange(slot_count) < elem_live[0]).astype(jnp.float32)
    rmask = residual * alive_mask[None, :]
    corner_weights = corner_table()
    derivative = derivative_matrix()
    corners = jnp.dot(corner_weights, rmask, precision=top_precision)
    coarse_partial = jax.ops.segment_sum(
        corners.reshape(-1), vertex_ids.reshape(-1), num_segments=coarse_inverse.shape[1]
    )
    coarse_rhs = lax.psum(coarse_partial, ("gx", "gy"))
    own_values = jnp.dot(coarse_inverse, coarse_rhs, precision=top_precision)
    coarse_sol = lax.all_gather(own_values, ("gx", "gy"), axis=0, tiled=True)
    smooth = fdm_solve(rmask.reshape(EDGE, EDGE, EDGE, -1), fdm_vectors, fdm_values).reshape(
        EDGE**3, -1
    )
    summed = face_sum(smooth, section_face, section_code, pipe_face, pipe_code)
    lifted = jnp.dot(corner_weights.T, coarse_sol[vertex_ids], precision=top_precision)
    direction = alive_mask[None, :] * (summed + lifted)
    applied, curvature_local = local_operator(direction, metric_diag, metric_cross, derivative)
    image = face_sum(applied, section_face, section_code, pipe_face, pipe_code)
    precond_local = jnp.sum(rmask * direction)
    norm_local = jnp.sum(rmask * rmask)
    precond_dot, curvature, old_norm = lax.psum(
        (precond_local, curvature_local, norm_local), ("gx", "gy")
    )
    step_length = precond_dot / curvature
    residual_out = rmask - step_length * image
    fresh_norm = lax.psum(jnp.sum(residual_out * residual_out), ("gx", "gy"))
    solution_out = alive_mask[None, :] * (solution + step_length * direction)
    norm_ratio = (fresh_norm / old_norm).reshape(1)
    return (solution_out, residual_out, norm_ratio)


def solution(mesh):
    placed = (
        P(None, ("gx", "gy")),
        P(None, ("gx", "gy")),
        P(None, None, ("gx", "gy")),
        P(None, None, ("gx", "gy")),
        P(None, None, None, ("gx", "gy")),
        P(None, None, ("gx", "gy")),
        P(None, ("gx", "gy")),
        P(("gx", "gy"), None),
        P(("gx", "gy")),
        P(("gx", "gy"), None, None),
        P(("gx", "gy"), None, None),
        P(("gx", "gy"), None, None),
        P(("gx", "gy"), None, None),
    )
    return jax.shard_map(
        on_device,
        mesh=mesh,
        in_specs=placed,
        out_specs=(P(None, ("gx", "gy")), P(None, ("gx", "gy")), P()),
        check_vma=False,
    )
```

profile of v0, /device:TPU:1, one launch (start us, length us, event | category | flops | bytes accessed | tf_op | source)
XLA Modules:
  0.0 567.3 jit_solution(12377010773833954774)
XLA Ops:
  0.7 0.9 slice_bitcast_fusion.120
  2.3 0.8 slice_bitcast_fusion.92
  3.8 1.0 broadcast_multiply_fusion.3
  6.8 2.3 copy.389
  9.0 2.5 reshape.1869
  12.5 1.1 gather_fusion.1
  14.6 7.6 %all-to-all-start = ((f32[16,1,1280]{2,1,0:T(1,128)}), f32[16,1,1280]{2,1,0:T(1,128)}, u32[]{:S(2)}, u32[]{:S(2)}) async-start(f32[16,1,1280]{2,1,0:T(1,128)} %reshape.1990), calls=%async_computation | async-start | bytes 163840 | tf_op jit(solution)/shard_map/all_to_all | solution.py:139
  23.7 2.5 collective-permute-start
  26.8 0.9 collective-permute-start.1
  30.1 5.9 %scatter_custom_fusion.1 = f32[8192]{0:T(1024)S(1)} fusion(s32[1024]{0:T(1024)S(1)} %bitcast.649, f32[1024]{0:T(1024)S(1)} %convolution_bitcast_fusion, f32[]{:T(128)} %constant.402.clone.1), kind=kCustom, calls=%fused_computation.199 | custom fusion | flops 1024 | bytes 32772 | tf_op jit(solution)/shard_map/scatter-add | solution.py:193
  36.1 108.5 %psum.35 = f32[8192]{0:T(1024)S(1)} all-reduce(f32[8192]{0:T(1024)S(1)} %scatter_custom_fusion.1), channel_id=1, replica_groups=mesh['gx'=32,'gy'=16] {'gx','gy'}, use_global_device_ids=true, to_apply=%region_2.5 | all-reduce | flops 8192 | bytes 65536 | tf_op jit(solution)/shard_map/psum | solution.py:196
  145.0 1.0 fusion.56
  145.9 1.0 fusion.55
  169.9 99.5 %all-reduce = f32[8192]{0:T(1024)S(1)} all-reduce(f32[8192]{0:T(1024)S(1)} %dynamic-update-slice.36), channel_id=1, replica_groups=mesh['gx'=32,'gy'=16] {'gx','gy'}, use_global_device_ids=true, to_apply=%add | all-reduce | flops 8192 | bytes 65536
  269.4 10.5 %gather_fusion = f32[1024]{0:T(1024)} fusion(f32[8192]{0:T(1024)S(1)} %all-reduce, s32[1024]{0:T(1024)S(1)} %fusion.40), kind=kCustom, calls=%fused_computation.4 | custom fusion | bytes 12288 | tf_op jit(solution)/shard_map/gather | solution.py:203
  280.6 1.6 reduce.26
  283.5 2.3 scatter_custom_fusion
  285.7 2.6 reshape.1876
  288.4 3.4 fusion.54
  291.8 1.9 copy.456
  293.6 0.8 copy.457
  294.4 1.3 copy.401
  295.7 1.2 copy.403
  296.9 1.2 copy.458
  298.1 1.2 copy.459
  299.4 0.9 fusion.25
  301.8 2.0 multiply_reduce_fusion
  304.4 1.5 multiply_add_fusion
  306.1 1.5 add_bitcast_fusion.1
  309.7 2.3 copy.428
  312.0 2.4 reshape.1886
  314.4 1.1 gather_fusion.3
  317.3 4.2 all-to-all-start.1
  322.3 1.8 collective-permute-start.2
  324.9 0.8 mul.2645
  326.7 0.8 mul.2661
  327.5 0.8 mul.2669
  339.6 2.9 add_reduce_fusion
  343.7 102.5 %all-reduce.2 = (f32[]{:T(128)}, f32[]{:T(128)}) all-reduce(f32[]{:T(128)} %get-tuple-element.150, f32[]{:T(128)S(6)} %add.970), channel_id=1, replica_groups=mesh['gx'=32,'gy'=16] {'gx','gy'}, use_global_device_ids=true, to_apply=%region_4.7 | all-reduce | flops 2 | bytes 16 | tf_op jit(solution)/shard_map/psum | solution.py:209
  447.6 1.7 add_multiply_fusion
  449.3 0.9 pad_maximum_fusion.1
  450.2 1.6 reduce.27
  453.1 2.5 scatter_custom_fusion.2
  455.7 2.6 reshape.1893
  458.3 2.9 fusion.53
  461.2 1.2 copy.462
  464.1 1.3 multiply_reduce_fusion.1
  465.4 99.4 %all-reduce.1 = (f32[]{:T(128)}, f32[]{:T(128)}) all-reduce(f32[]{:T(128)} %get-tuple-element.156, f32[]{:T(128)} %get-tuple-element.149), channel_id=1, replica_groups=mesh['gx'=32,'gy'=16] {'gx','gy'}, use_global_device_ids=true, to_apply=%region_11.14 | all-reduce | flops 2 | bytes 16 | tf_op jit(solution)/shard_map/psum | solution.py:214
  (499 shorter events, 55.4 us)
Async XLA Ops:
  0.6 147.6 %copy-start = (f32[16,8192]{1,0:T(8,128)S(1)}, f32[16,8192]{1,0:T(8,128)}, u32[]{:S(2)}) copy-start(f32[16,8192]{1,0:T(8,128)} %param.48) | copy-start | bytes 1572868
  9.0 13.9 %copy-start.124 = (s32[1,2,64]{2,1,0:T(2,128)S(1)}, s32[1,2,64]{2,1,0:T(2,128)}, u32[]{:S(2)}) copy-start(s32[1,2,64]{2,1,0:T(2,128)} %param.53) | copy-start | bytes 1540
  9.0 21.1 %copy-start.121 = (s32[8,128]{1,0:T(8,128)S(1)}, s32[8,128]{1,0:T(8,128)}, u32[]{:S(2)}) copy-start(s32[8,128]{1,0:T(8,128)} %param.47) | copy-start | bytes 12292
  9.0 135.9 %copy-start.2 = (bf16[3,512,128]{2,1,0:T(8,128)(2,1)S(1)}, bf16[3,512,128]{2,1,0:T(8,128)(2,1)}, u32[]{:S(2)}) copy-start(bf16[3,512,128]{2,1,0:T(8,128)(2,1)} %param.44) | copy-start | bytes 1179652
  11.5 134.5 %copy-start.1 = (bf16[3,512,128]{2,1,0:T(8,128)(2,1)S(1)}, bf16[3,512,128]{2,1,0:T(8,128)(2,1)}, u32[]{:S(2)}) copy-start(bf16[3,512,128]{2,1,0:T(8,128)(2,1)} %param.43) | copy-start | bytes 1179652
  12.5 134.4 %copy-start.110 = (s32[1024]{0:T(1024)}, s32[1024]{0:T(1024)S(1)}, u32[]{:S(2)}) copy-start(s32[1024]{0:T(1024)S(1)} %get-tuple-element.373) | copy-start | bytes 12292
  14.6 265.5 %all-to-all-start = ((f32[16,1,1280]{2,1,0:T(1,128)}), f32[16,1,1280]{2,1,0:T(1,128)}, u32[]{:S(2)}, u32[]{:S(2)}) async-start(f32[16,1,1280]{2,1,0:T(1,128)} %reshape.1990), calls=%async_computation | async-start | bytes 163840 | tf_op jit(solution)/shard_map/all_to_all | solution.py:139
  23.5 256.5 %copy-start.66 = (pred[128]{0:T(512)(128)(4,1)}, pred[128]{0:T(512)(128)(4,1)S(1)}, u32[]{:S(2)}) copy-start(pred[128]{0:T(512)(128)(4,1)S(1)} %get-tuple-element.360) | copy-start | bytes 388
  23.7 256.2 %collective-permute-start = (f32[64,1,64]{2,0,1:T(8,128)S(1)}, f32[64,1,64]{2,0,1:T(8,128)S(1)}, u32[]{:S(2)}, u32[]{:S(2)}) collective-permute-start(f32[64,1,64]{2,0,1:T(8,128)S(1)} %copy.454), channel_id=1, source_target_pairs={{0,16},{16,32},{32,48},{48,64},{64,80},{80,96},{96,112},{112,128},... | collective-permute-start | bytes 49160 | tf_op jit(solution)/shard_map/ppermute | solution.py:18
  26.8 253.1 %collective-permute-start.1 = (f32[64,1,64]{2,0,1:T(8,128)}, f32[64,1,64]{2,0,1:T(8,128)S(1)}, u32[]{:S(2)}, u32[]{:S(2)}) collective-permute-start(f32[64,1,64]{2,0,1:T(8,128)} %copy.455), channel_id=1, source_target_pairs={{16,0},{32,16},{48,32},{64,48},{80,64},{96,80},{112,96},{128,112},... | collective-permute-start | bytes 49160 | tf_op jit(solution)/shard_map/ppermute | solution.py:21
  144.9 19.5 %copy-start.42 = (f32[8]{0:T(128)}, f32[8]{0:T(128)S(1)}, u32[]{:S(2)}) copy-start(f32[8]{0:T(128)S(1)} %get-tuple-element.346) | copy-start | bytes 100
  144.9 20.1 %copy-start.56 = (f32[8]{0:T(128)}, f32[8]{0:T(128)S(1)}, u32[]{:S(2)}) copy-start(f32[8]{0:T(128)S(1)} %get-tuple-element.353) | copy-start | bytes 100
  144.9 20.8 %copy-start.54 = (f32[8]{0:T(128)}, f32[8]{0:T(128)S(1)}, u32[]{:S(2)}) copy-start(f32[8]{0:T(128)S(1)} %get-tuple-element.352) | copy-start | bytes 100
  144.9 21.4 %copy-start.52 = (f32[8]{0:T(128)}, f32[8]{0:T(128)S(1)}, u32[]{:S(2)}) copy-start(f32[8]{0:T(128)S(1)} %get-tuple-element.351) | copy-start | bytes 100
  144.9 22.1 %copy-start.50 = (f32[8]{0:T(128)}, f32[8]{0:T(128)S(1)}, u32[]{:S(2)}) copy-start(f32[8]{0:T(128)S(1)} %get-tuple-element.350) | copy-start | bytes 100
  144.9 22.8 %copy-start.48 = (f32[8]{0:T(128)}, f32[8]{0:T(128)S(1)}, u32[]{:S(2)}) copy-start(f32[8]{0:T(128)S(1)} %get-tuple-element.349) | copy-start | bytes 100
  144.9 23.5 %copy-start.46 = (f32[8]{0:T(128)}, f32[8]{0:T(128)S(1)}, u32[]{:S(2)}) copy-start(f32[8]{0:T(128)S(1)} %get-tuple-element.348) | copy-start | bytes 100
  145.0 24.1 %copy-start.44 = (f32[8]{0:T(128)}, f32[8]{0:T(128)S(1)}, u32[]{:S(2)}) copy-start(f32[8]{0:T(128)S(1)} %get-tuple-element.347) | copy-start | bytes 100
  152.5 127.5 %copy-start.83 = (pred[128]{0:T(512)(128)(4,1)S(1)}, pred[128]{0:T(512)(128)(4,1)}, u32[]{:S(2)}) copy-start(pred[128]{0:T(512)(128)(4,1)} %get-tuple-element.361) | copy-start | bytes 388
  152.6 127.5 %copy-start.117 = (pred[128]{0:T(512)(128)(4,1)S(1)}, pred[128]{0:T(512)(128)(4,1)}, u32[]{:S(2)}) copy-start(pred[128]{0:T(512)(128)(4,1)} %get-tuple-element.359) | copy-start | bytes 388
  165.0 117.4 %copy-start.122 = (pred[16]{0:T(512)(128)(4,1)S(1)}, pred[16]{0:T(512)(128)(4,1)}, u32[]{:S(2)}) copy-start(pred[16]{0:T(512)(128)(4,1)} %iota_compare_fusion.2) | copy-start | bytes 52
  269.4 13.6 %copy-start.64 = (pred[320]{0:T(512)(128)(4,1)S(1)}, pred[320]{0:T(512)(128)(4,1)}, u32[]{:S(2)}) copy-start(pred[320]{0:T(512)(128)(4,1)} %get-tuple-element.355) | copy-start | bytes 964
  269.4 13.8 %copy-start.73 = (pred[320]{0:T(512)(128)(4,1)S(1)}, pred[320]{0:T(512)(128)(4,1)}, u32[]{:S(2)}) copy-start(pred[320]{0:T(512)(128)(4,1)} %get-tuple-element.356) | copy-start | bytes 964
  269.4 13.8 %copy-start.111 = (pred[320]{0:T(512)(128)(4,1)S(1)}, pred[320]{0:T(512)(128)(4,1)}, u32[]{:S(2)}) copy-start(pred[320]{0:T(512)(128)(4,1)} %get-tuple-element.354) | copy-start | bytes 964
  317.3 132.9 %all-to-all-start.1 = ((f32[16,1,1280]{2,1,0:T(1,128)}), f32[16,1,1280]{2,1,0:T(1,128)}, u32[]{:S(2)}, u32[]{:S(2)}) async-start(f32[16,1,1280]{2,1,0:T(1,128)} %reshape.1992), calls=%async_computation.1 | async-start | bytes 163840 | tf_op jit(solution)/shard_map/all_to_all | solution.py:139
  321.4 17.7 %copy-start.19 = (f32[1,8,8,128]{3,0,2,1:T(1,128)S(1)}, f32[1,8,8,128]{3,0,2,1:T(1,128)}, u32[]{:S(2)}) copy-start(f32[1,8,8,128]{3,0,2,1:T(1,128)} %copy-done.18) | copy-start | bytes 98308
  322.3 127.0 %collective-permute-start.2 = (f32[64,1,64]{2,0,1:T(8,128)}, f32[64,1,64]{2,0,1:T(8,128)}, u32[]{:S(2)}, u32[]{:S(2)}) collective-permute-start(f32[64,1,64]{2,0,1:T(8,128)} %copy.460), channel_id=1, source_target_pairs={{0,16},{16,32},{32,48},{48,64},{64,80},{80,96},{96,112},{112,128},... | collective-permute-start | bytes 49160 | tf_op jit(solution)/shard_map/ppermute | solution.py:18
  324.1 15.1 %copy-start.17 = (f32[1,8,8,128]{3,0,2,1:T(1,128)S(1)}, f32[1,8,8,128]{3,0,2,1:T(1,128)}, u32[]{:S(2)}) copy-start(f32[1,8,8,128]{3,0,2,1:T(1,128)} %copy-done.16) | copy-start | bytes 98308
  324.8 124.5 %collective-permute-start.3 = (f32[64,1,64]{2,0,1:T(8,128)}, f32[64,1,64]{2,0,1:T(8,128)}, u32[]{:S(2)}, u32[]{:S(2)}) collective-permute-start(f32[64,1,64]{2,0,1:T(8,128)} %copy.461), channel_id=1, source_target_pairs={{16,0},{32,16},{48,32},{64,48},{80,64},{96,80},{112,96},{128,112},... | collective-permute-start | bytes 49160 | tf_op jit(solution)/shard_map/ppermute | solution.py:21
  324.8 14.4 %copy-start.15 = (f32[1,8,8,128]{3,0,2,1:T(1,128)S(1)}, f32[1,8,8,128]{3,0,2,1:T(1,128)}, u32[]{:S(2)}) copy-start(f32[1,8,8,128]{3,0,2,1:T(1,128)} %copy-done.14) | copy-start | bytes 98308
  324.9 14.4 %copy-start.13 = (f32[1,8,8,128]{3,0,2,1:T(1,128)S(1)}, f32[1,8,8,128]{3,0,2,1:T(1,128)}, u32[]{:S(2)}) copy-start(f32[1,8,8,128]{3,0,2,1:T(1,128)} %copy-done.12) | copy-start | bytes 98308
  325.7 13.6 %copy-start.86 = (f32[512]{0:T(512)S(1)}, f32[512]{0:T(512)}, u32[]{:S(2)}) copy-start(f32[512]{0:T(512)} %mul.2626) | copy-start | bytes 6148
  325.7 13.6 %copy-start.87 = (f32[512]{0:T(512)S(1)}, f32[512]{0:T(512)}, u32[]{:S(2)}) copy-start(f32[512]{0:T(512)} %mul.2634) | copy-start | bytes 6148
  325.7 13.6 %copy-start.88 = (f32[512]{0:T(512)S(1)}, f32[512]{0:T(512)}, u32[]{:S(2)}) copy-start(f32[512]{0:T(512)} %mul.2642) | copy-start | bytes 6148
  325.7 13.6 %copy-start.89 = (f32[512]{0:T(512)S(1)}, f32[512]{0:T(512)}, u32[]{:S(2)}) copy-start(f32[512]{0:T(512)} %mul.2650) | copy-start | bytes 6148
  325.7 13.6 %copy-start.90 = (f32[512]{0:T(512)S(1)}, f32[512]{0:T(512)}, u32[]{:S(2)}) copy-start(f32[512]{0:T(512)} %mul.2658) | copy-start | bytes 6148
  325.7 13.6 %copy-start.91 = (f32[512]{0:T(512)S(1)}, f32[512]{0:T(512)}, u32[]{:S(2)}) copy-start(f32[512]{0:T(512)} %mul.2666) | copy-start | bytes 6148
  325.7 13.6 %copy-start.92 = (f32[512]{0:T(512)S(1)}, f32[512]{0:T(512)}, u32[]{:S(2)}) copy-start(f32[512]{0:T(512)} %mul.2674) | copy-start | bytes 6148
  325.7 13.6 %copy-start.93 = (f32[512]{0:T(512)S(1)}, f32[512]{0:T(512)}, u32[]{:S(2)}) copy-start(f32[512]{0:T(512)} %mul.2682) | copy-start | bytes 6148
  325.7 13.6 %copy-start.94 = (f32[512]{0:T(512)S(1)}, f32[512]{0:T(512)}, u32[]{:S(2)}) copy-start(f32[512]{0:T(512)} %mul.2690) | copy-start | bytes 6148
  339.5 108.0 %copy-start.72 = (f32[128]{0:T(128)S(1)}, f32[128]{0:T(128)}, u32[]{:S(2)}) copy-start(f32[128]{0:T(128)} %copy-done.71) | copy-start | bytes 1540
  339.5 110.6 %copy-start.67 = (pred[128]{0:T(512)(128)(4,1)S(1)}, pred[128]{0:T(512)(128)(4,1)}, u32[]{:S(2)}) copy-start(pred[128]{0:T(512)(128)(4,1)} %copy-done.66) | copy-start | bytes 388
  339.6 110.6 %copy-start.84 = (pred[128]{0:T(512)(128)(4,1)S(1)}, pred[128]{0:T(512)(128)(4,1)}, u32[]{:S(2)}) copy-start(pred[128]{0:T(512)(128)(4,1)} %get-tuple-element.361) | copy-start | bytes 388
  339.6 110.6 %copy-start.118 = (pred[128]{0:T(512)(128)(4,1)S(1)}, pred[128]{0:T(512)(128)(4,1)}, u32[]{:S(2)}) copy-start(pred[128]{0:T(512)(128)(4,1)} %get-tuple-element.359) | copy-start | bytes 388
  339.6 112.4 %copy-start.123 = (pred[16]{0:T(512)(128)(4,1)S(1)}, pred[16]{0:T(512)(128)(4,1)}, u32[]{:S(2)}) copy-start(pred[16]{0:T(512)(128)(4,1)} %iota_compare_fusion.2) | copy-start | bytes 52
  342.5 110.2 %copy-start.65 = (pred[320]{0:T(512)(128)(4,1)S(1)}, pred[320]{0:T(512)(128)(4,1)}, u32[]{:S(2)}) copy-start(pred[320]{0:T(512)(128)(4,1)} %get-tuple-element.355) | copy-start | bytes 964
  342.5 110.4 %copy-start.74 = (pred[320]{0:T(512)(128)(4,1)S(1)}, pred[320]{0:T(512)(128)(4,1)}, u32[]{:S(2)}) copy-start(pred[320]{0:T(512)(128)(4,1)} %get-tuple-element.356) | copy-start | bytes 964
  342.5 110.4 %copy-start.112 = (pred[320]{0:T(512)(128)(4,1)S(1)}, pred[320]{0:T(512)(128)(4,1)}, u32[]{:S(2)}) copy-start(pred[320]{0:T(512)(128)(4,1)} %get-tuple-element.354) | copy-start | bytes 964
  (84 other events, 478.1 us)
where the time goes:
time: 570 us; the launch traced here: 567 us
  blocking collectives  410 us (72%)
  local copies, waits for them, and re-layouts  94 us (16%)
  other arithmetic  34.3 us (6%)
  starting transfers between devices  17 us (3%)
  between operations  9.18 us (2%)
    psum x1, blocking collectives, on_device(): coarse_rhs = lax.psum(coarse_partial, ('gx', 'gy'))  109 us
    psum x1, blocking collectives, on_device(): lax.psum((precond_local, curvature_local, norm_local), ('gx', 'gy'))  102 us
    unnamed x1, blocking collectives  99.5 us
    psum x1, blocking collectives, on_device(): fresh_norm = lax.psum(jnp.sum(residual_out * residual_out), ('gx', 'gy'))  99.4 us
    mul x78, local copies, waits for them, and re-layouts, contract(): total = total + matrices[index][:, None, None, :] * moved[index][None]  28.3 us
    unnamed x280, local copies, waits for them, and re-layouts  12 us
    all_to_all x2, starting transfers between devices, face_sum(): lax.all_to_all(outgoing, 'gy', split_axis=1, concat_axis=1, tiled=True)  11.8 us
  transfers between devices with their start and end apart: 6, of which 0 were waited for; matrix products, arithmetic and copies ran while one was open for 12% of the time, Pallas kernels for 0%

commit v1 on v0

v1 whole, which is shorter than its diff:
```python
import functools

import numpy as np
import jax
import jax.numpy as jnp
from jax import lax
from jax.experimental import pallas as pl
from jax.experimental.pallas import tpu as pltpu
from jax.sharding import PartitionSpec as P

EDGE = 8
LANES = 128
POINTS = 512
F32 = jnp.float32
BF16 = jnp.bfloat16
MESH = pl.DeviceIdType.MESH
NT = (((1,), (1,)), ((), ()))

ROWS = 320
FIRST = 32
PEER_ROW = 64
PEER_ROWS = 24
SPARE = 184
PIPE_ROW = 192
PIPE_ROWS = 64
SENT_ROWS = 5 * PEER_ROWS + 2 * PIPE_ROWS
USED = ROWS - FIRST


def node_points():
    return -np.cos(np.pi * np.arange(EDGE) / (EDGE - 1))


def derivative_matrix():
    t = node_points()
    c = np.where((np.arange(EDGE) == 0) | (np.arange(EDGE) == EDGE - 1), 2.0, 1.0)
    d = np.zeros((EDGE, EDGE))
    for a in range(EDGE):
        for b in range(EDGE):
            if a != b:
                d[a, b] = c[a] / c[b] * (-1.0) ** (a + b) / (t[a] - t[b])
    for a in range(EDGE):
        d[a, a] = -np.sum(d[a])
    return d


def halves(matrix):
    front, back = matrix[:4, :4], matrix[:4, ::-1][:, :4]
    return (front + back) / 2, (front - back) / 2


D_EVEN, D_ODD = halves(derivative_matrix())
T_EVEN, T_ODD = halves(derivative_matrix().T)
HATS = np.stack([(1.0 - node_points()) / 2, (1.0 + node_points()) / 2])


def mirrored(even, odd, u):
    total = [u[m] + u[7 - m] for m in range(4)]
    apart = [u[m] - u[7 - m] for m in range(4)]
    front, back = [], []
    for a in range(4):
        e = float(even[a, 0]) * total[0]
        o = float(odd[a, 0]) * apart[0]
        for m in range(1, 4):
            e = e + float(even[a, m]) * total[m]
            o = o + float(odd[a, m]) * apart[m]
        front.append(o + e)
        back.append(o - e)
    return front + back[::-1]


def split(x):
    high = x.astype(BF16)
    return high, (x - high.astype(F32)).astype(BF16)


def iota(shape, dim):
    return lax.broadcasted_iota(jnp.int32, shape, dim)


def kernel(
    n_x,
    n_y,
    live_ref,
    vid_ref,
    eig_ref,
    sface_ref,
    scode_ref,
    pface_ref,
    pcode_ref,
    sol_hbm,
    res_hbm,
    diag_hbm,
    cross_hbm,
    fdm_hbm,
    inv_hbm,
    sol_out,
    res_out,
    ratio_out,
    sol_in,
    rm,
    diag,
    cross,
    fdm,
    inv,
    buf_a,
    buf_b,
    field,
    turned,
    turned2,
    grad1,
    direction,
    x_one,
    y_one,
    h_one,
    part,
    rc1,
    own2,
    rc2,
    own3,
    rc3,
    own4,
    rc4,
    own5,
    rc5,
    coarse,
    idm,
    cdm,
    onehot,
    masks,
    perm,
    faces,
    out1,
    inc1,
    out2,
    inc2,
    picked,
    own_a,
    rc_a,
    own_b,
    rc_b,
    in_sem,
    send_sem,
    recv_sem,
):
    x, y = lax.axis_index("gx"), lax.axis_index("gy")
    offsets = (1, n_y - 1, 2, n_y - 2, n_y // 2)
    back_to = (1, 0, 3, 2, 4)

    loads = [
        pltpu.make_async_copy(s, d, in_sem.at[i])
        for i, (s, d) in enumerate(
            [(res_hbm, rm), (fdm_hbm, fdm), (inv_hbm, inv), (diag_hbm, diag), (cross_hbm, cross), (sol_hbm, sol_in)]
        )
    ]
    for load in loads:
        load.start()

    barrier = pltpu.get_barrier_semaphore()

    def greet(axis, me, n):
        def body(k, c):
            pl.semaphore_signal(barrier, inc=1, device_id={axis: lax.rem(me + k, n)}, device_id_type=MESH)
            return c

        lax.fori_loop(1, n, body, 0)

    greet("gy", y, n_y)
    greet("gx", x, n_x)

    def send_all(axis, me, n, source, landing, phase):
        def body(k, c):
            target = lax.rem(me + k, n)
            pltpu.make_async_remote_copy(
                src_ref=source(target),
                dst_ref=landing.at[me],
                send_sem=send_sem.at[phase],
                recv_sem=recv_sem.at[phase],
                device_id={axis: target},
                device_id_type=MESH,
            ).start()
            return c

        lax.fori_loop(1, n, body, 0)

    def await_all(sem, landing, n):
        some = landing.at[pl.ds(0, n - 1)]
        pltpu.make_async_copy(some, some, sem).wait()

    alive = (iota((1, LANES), 1) < live_ref[0]).astype(F32)
    lane = iota((1, LANES), 1)
    sub8 = iota((EDGE, 1), 0)
    hat_rows = []
    for c in range(2):
        h = jnp.zeros((EDGE, 1), F32)
        for k in range(EDGE):
            h = jnp.where(sub8 == k, float(HATS[c, k]), h)
        hat_rows.append(h)

    inc1[pl.ds(SPARE, 8), :] = jnp.zeros((8, LANES), F32)
    inc2[pl.ds(SPARE, 8), :] = jnp.zeros((8, LANES), F32)
    loads[0].wait()
    along_i = [None, None]
    for i in range(EDGE):
        slab = rm[pl.ds(64 * i, 64), :] * alive
        rm[pl.ds(64 * i, 64), :] = slab
        for c in range(2):
            term = float(HATS[c, i]) * slab
            along_i[c] = term if i == 0 else along_i[c] + term
    high_iota = iota((64, LANES), 0)
    low_iota = iota((LANES, LANES), 0)
    for ci in range(2):
        for cj in range(2):
            plane = float(HATS[cj, 0]) * along_i[ci][0:8]
            for j in range(1, EDGE):
                plane = plane + float(HATS[cj, j]) * along_i[ci][8 * j : 8 * j + 8]
            for ck in range(2):
                c = 4 * ci + 2 * cj + ck
                value = jnp.sum(plane * hat_rows[ck], axis=0, keepdims=True)
                ids = vid_ref[c : c + 1, :]
                at = pl.ds(c * LANES, LANES)
                here = (high_iota == (ids >> 7)).astype(F32)
                h_one[:, at] = here
                high, low = split(here * value)
                x_one[0:64, at] = high
                x_one[64:128, at] = low
                y_one[:, at] = (low_iota == (ids & 127)).astype(F32).astype(BF16)
    both = lax.dot_general(x_one[...], y_one[...], NT, preferred_element_type=F32)
    partial = both[0:64] + both[64:128]
    rows1 = 64 // n_y
    for q in range(n_y):
        part[q] = partial[rows1 * q : rows1 * q + rows1]

    pl.semaphore_wait(barrier, n_x + n_y - 2)

    send_all("gy", y, n_y, lambda t: part.at[t], rc1, 0)
    rc1[y] = part[y]

    def column(row, rows, swap=0):
        width = row.shape[1]
        diagonal = (iota((rows, width), 0) ^ swap) == iota((rows, width), 1)
        kept = jnp.where(diagonal, row.astype(F32) + 1.0, 0.0)
        return jnp.broadcast_to(jnp.sum(kept, axis=1, keepdims=True) - 1.0, (rows, LANES))

    idm[pl.ds(0, 32), :] = column(sface_ref[0, pl.ds(y, 1), :], 32, 1)
    idm[pl.ds(32, 32), :] = column(sface_ref[0, pl.ds(y, 1), :], 32)
    cdm[pl.ds(0, 32), :] = column(scode_ref[0, pl.ds(y, 1), :], 32)
    for g in range(5):
        peer = lax.rem(y + offsets[g], n_y)
        at = PEER_ROW + PEER_ROWS * g
        idm[pl.ds(at, PEER_ROWS), :] = column(sface_ref[0, pl.ds(peer, 1), :], PEER_ROWS)
        cdm[pl.ds(at - FIRST, PEER_ROWS), :] = column(scode_ref[0, pl.ds(peer, 1), :], PEER_ROWS)
    idm[pl.ds(SPARE, 8), :] = jnp.full((8, LANES), -1.0, F32)
    cdm[pl.ds(SPARE - FIRST, 8), :] = jnp.full((8, LANES), -1.0, F32)
    for s in range(2):
        at = PIPE_ROW + PIPE_ROWS * s
        idm[pl.ds(at, PIPE_ROWS), :] = column(pface_ref[0, s : s + 1, :], PIPE_ROWS)
        cdm[pl.ds(at - FIRST, PIPE_ROWS), :] = column(pcode_ref[0, s : s + 1, :], PIPE_ROWS)
    ids = idm[...]
    for f in range(6):
        onehot[:, pl.ds(f * LANES, LANES)] = (ids == (6 * lane + f).astype(F32)).astype(F32).astype(BF16)
    codes = cdm[...]
    half = (lane >> 6).astype(F32)
    for p in range(4):
        masks[:, pl.ds(p * LANES, LANES)] = (codes == 2.0 * p + half).astype(F32).astype(BF16)
    grid_row = iota((LANES, LANES), 0)
    grid_lane = iota((LANES, LANES), 1)
    first, second = (grid_row & 63) >> 3, grid_row & 7
    flip = 7 * (grid_lane >> 6)
    for t in range(8):
        a, b = (second, first) if t % 4 >= 2 else (first, second)
        b = b ^ 7 if t % 2 == 1 else b
        source = 8 * (a ^ flip) + b
        fits = (source == (grid_lane & 63)) & ((grid_row < 64) if t < 4 else (grid_row >= 64))
        perm[:, pl.ds(t * LANES, LANES)] = fits.astype(F32).astype(BF16)

    await_all(recv_sem.at[0], rc1, n_y)
    mine = jnp.sum(rc1[...], axis=0)
    own2[...] = mine
    rc2[x] = mine
    send_all("gx", x, n_x, lambda t: own2, rc2, 1)

    def sum_of(coef, slabs, a):
        total = coef(0, a) * slabs(0)
        for m in range(1, EDGE):
            total = total + coef(m, a) * slabs(m)
        return total

    def per_row(body):
        def step(a, c):
            body(a)
            return c

        lax.fori_loop(0, EDGE, step, 0)

    def slab_i(ref):
        return lambda m: ref[pl.ds(pl.multiple_of(64 * m, 64), 64), :]

    def slab_j(ref):
        cube = ref.reshape(EDGE, EDGE, EDGE, LANES)
        return lambda m: cube[:, m].reshape(64, LANES)

    def forward(d):
        return lambda m, a: fdm[d, m, pl.ds(a, 1), :]

    def backward(d):
        return lambda m, a: fdm[d, a, m : m + 1, :]

    def put_i(ref, a, value):
        ref[pl.ds(pl.multiple_of(64 * a, 64), 64), :] = value

    def put_j(ref, a, value):
        ref.reshape(EDGE, EDGE, EDGE, LANES)[:, pl.ds(a, 1)] = value.reshape(EDGE, 1, EDGE, LANES)

    loads[1].wait()
    per_row(lambda a: put_i(buf_a, a, sum_of(forward(0), slab_i(rm), a)))
    per_row(lambda a: put_j(buf_b, a, sum_of(forward(1), slab_j(buf_a), a)))
    for k in range(EDGE):
        turned[pl.ds(64 * k, 64), :] = buf_b[pl.ds(k, 64, stride=EDGE), :]
    base = jnp.concatenate([eig_ref[0, a : a + 1, :] + eig_ref[1] for a in range(EDGE)], axis=0)
    buf_a[pl.ds(0, 64), :] = base

    def spectral(a):
        value = sum_of(forward(2), slab_i(turned), a)
        put_i(buf_b, a, value / (buf_a[pl.ds(0, 64), :] + eig_ref[2, pl.ds(a, 1), :]))

    per_row(spectral)

    await_all(recv_sem.at[1], rc2, n_x)
    mine = jnp.sum(rc2[...], axis=0)
    own3[...] = mine
    rc3[y] = mine
    send_all("gy", y, n_y, lambda t: own3, rc3, 2)

    per_row(lambda a: put_i(turned, a, sum_of(backward(2), slab_i(buf_b), a)))
    for k in range(EDGE):
        buf_a[pl.ds(k, 64, stride=EDGE), :] = turned[pl.ds(64 * k, 64), :]
    per_row(lambda a: put_j(buf_b, a, sum_of(backward(1), slab_j(buf_a), a)))
    per_row(lambda a: put_i(field, a, sum_of(backward(0), slab_i(buf_b), a)))

    def face_of(ref, f):
        if f < 2:
            return ref[pl.ds(448 * f, 64), :]
        if f < 4:
            return slab_j(ref)(7 * (f - 2))
        return ref[pl.ds(7 * (f - 4), 64, stride=EDGE), :]

    def send_faces(ref, out, inc, phase):
        for f in range(6):
            high, low = split(face_of(ref, f))
            faces[0:64, pl.ds(f * LANES, LANES)] = high
            faces[64:128, pl.ds(f * LANES, LANES)] = low
        found = lax.dot_general(onehot[...], faces[...], NT, preferred_element_type=F32)
        found = found + pltpu.roll(found, 64, 1)
        out[...] = found
        inc[pl.ds(FIRST, 32), :] = found[0:32]
        hops = [
            (PEER_ROW + PEER_ROWS * g, PEER_ROW + PEER_ROWS * back_to[g], PEER_ROWS, {"gy": lax.rem(y + offsets[g], n_y)})
            for g in range(5)
        ] + [
            (
                PIPE_ROW + PIPE_ROWS * s,
                PIPE_ROW + PIPE_ROWS * (1 - s),
                PIPE_ROWS,
                {"gx": lax.rem(x + n_x - 1 + 2 * s, n_x)},
            )
            for s in range(2)
        ]
        for start, land, count, target in hops:
            pltpu.make_async_remote_copy(
                src_ref=out.at[pl.ds(start, count)],
                dst_ref=inc.at[pl.ds(land, count)],
                send_sem=send_sem.at[phase],
                recv_sem=recv_sem.at[phase],
                device_id=target,
                device_id_type=MESH,
            ).start()

    def await_faces(sem, inc):
        some = inc.at[pl.ds(0, SENT_ROWS)]
        pltpu.make_async_copy(some, some, sem).wait()

    def place_faces(ref, inc):
        high, low = split(inc[pl.ds(FIRST, USED), :])
        for p in range(4):
            mask = masks[:, pl.ds(p * LANES, LANES)]
            picked[:, pl.ds(p * LANES, LANES)] = high * mask
            picked[:, pl.ds((p + 4) * LANES, LANES)] = low * mask
        across = lax.dot_general(perm[...], picked[...], NT, preferred_element_type=F32)
        extra = jnp.dot(across.astype(BF16), onehot[pl.ds(FIRST, USED), :], preferred_element_type=F32)
        extra = extra[0:64] + extra[64:128]
        cube = ref.reshape(EDGE, EDGE, EDGE, LANES)
        for f in range(6):
            more = extra[:, f * LANES : (f + 1) * LANES]
            if f < 2:
                ref[pl.ds(448 * f, 64), :] += more
            elif f < 4:
                cube[:, 7 * (f - 2)] += more.reshape(EDGE, EDGE, LANES)
            else:
                at = pl.ds(7 * (f - 4), 64, stride=EDGE)
                ref[at, :] = ref[at, :] + more

    send_faces(field, out1, inc1, 7)

    await_all(recv_sem.at[2], rc3, n_y)
    loads[2].wait()

    def rows_times(q, acc):
        for r in range(rows1):
            at = pl.ds(pl.multiple_of((q * rows1 + r) * LANES, LANES), LANES)
            acc = acc + inv[:, at] * rc3[q, r : r + 1, :]
        return acc

    acc = lax.fori_loop(0, n_y, rows_times, jnp.zeros((16, LANES), F32))
    own_values = jnp.sum(acc, axis=1, keepdims=True)
    spot = iota((16, LANES), 1) == 16 * lax.rem(y, 8) + iota((16, LANES), 0)
    row = jnp.sum(jnp.where(spot, own_values, 0.0), axis=0, keepdims=True)
    own4[...] = row
    rc4[y] = row

    send_all("gy", y, n_y, lambda t: own4, rc4, 3)
    await_faces(recv_sem.at[7], inc1)
    place_faces(field, inc1)

    await_all(recv_sem.at[3], rc4, n_y)
    pair = jnp.concatenate([jnp.sum(rc4[0:8], axis=0), jnp.sum(rc4[8:16], axis=0)], axis=0)
    own5[...] = pair
    rc5[x] = pair
    send_all("gx", x, n_x, lambda t: own5, rc5, 4)
    loads[3].wait()
    loads[4].wait()
    await_all(recv_sem.at[4], rc5, n_x)
    for q in range(n_x):
        coarse[pl.ds(2 * q, 2), :] = rc5[q]

    high, low = split(coarse[...])
    at_low = jnp.dot(jnp.concatenate([high, low], axis=0), y_one[...], preferred_element_type=F32)
    corner = jnp.sum((at_low[0:64] + at_low[64:128]) * h_one[...], axis=0, keepdims=True)
    planes = []
    for ci in range(2):
        lines = []
        for cj in range(2):
            at = (4 * ci + 2 * cj) * LANES
            lines.append(hat_rows[0] * corner[:, at : at + LANES] + hat_rows[1] * corner[:, at + LANES : at + 2 * LANES])
        planes.append(
            jnp.concatenate(
                [float(HATS[0, j]) * lines[0] + float(HATS[1, j]) * lines[1] for j in range(EDGE)], axis=0
            )
        )
    for i in range(EDGE):
        at = pl.ds(64 * i, 64)
        lifted = float(HATS[0, i]) * planes[0] + float(HATS[1, i]) * planes[1]
        direction[at, :] = alive * (field[at, :] + lifted)

    def take(ref, start, stride):
        return [ref[pl.ds(pl.multiple_of(start + stride * m, 8), 8), :] for m in range(EDGE)]

    def along_first(j, c):
        result = mirrored(D_EVEN, D_ODD, take(direction, 8 * j, 64))
        for a in range(EDGE):
            grad1[pl.ds(pl.multiple_of(64 * a + 8 * j, 8), 8), :] = result[a]
        return c

    lax.fori_loop(0, EDGE, along_first, 0)

    def turn(values, ref):
        for m in range(EDGE):
            ref[pl.ds(EDGE * m, EDGE), :] = values[m]
        return [ref[pl.ds(m, EDGE, stride=EDGE), :] for m in range(EDGE)]

    def middle(i, sums):
        curve, dots = sums
        start = pl.multiple_of(64 * i, 64)
        slab = pl.ds(start, 64)
        d = take(direction, start, 8)
        across = turn(d, turned.at[pl.ds(0, 64)])
        g3 = turn(mirrored(D_EVEN, D_ODD, across), turned.at[pl.ds(64, 64)])
        g2 = mirrored(D_EVEN, D_ODD, d)
        g1 = take(grad1, start, 8)
        m = [diag[q, slab, :].astype(F32) for q in range(3)] + [cross[q, slab, :].astype(F32) for q in range(3)]
        f2, f3 = [], []
        for j in range(EDGE):
            rr, ss, tt, rs, rt, st = [q[8 * j : 8 * j + 8] for q in m]
            u = rr * g1[j] + rs * g2[j] + rt * g3[j]
            v = rs * g1[j] + ss * g2[j] + st * g3[j]
            w = rt * g1[j] + st * g2[j] + tt * g3[j]
            curve = curve + (g1[j] * u + g2[j] * v) + (g3[j] * w + d[j] * d[j])
            grad1[pl.ds(start + 8 * j, 8), :] = u
            f2.append(v)
            f3.append(w)
        dots = dots + jnp.sum((rm[slab, :] * direction[slab, :]).reshape(EDGE, EDGE, LANES), axis=0)
        b3 = turn(mirrored(T_EVEN, T_ODD, turn(f3, turned2.at[pl.ds(0, 64)])), turned2.at[pl.ds(64, 64)])
        b2 = mirrored(T_EVEN, T_ODD, f2)
        for j in range(EDGE):
            field[pl.ds(start + 8 * j, 8), :] = (b2[j] + b3[j]) + d[j]
        return curve, dots

    zero = jnp.zeros((EDGE, LANES), F32)
    curve, dots = lax.fori_loop(0, EDGE, middle, (zero, zero))

    def back_first(j, c):
        result = mirrored(T_EVEN, T_ODD, take(grad1, 8 * j, 64))
        for a in range(EDGE):
            at = pl.ds(pl.multiple_of(64 * a + 8 * j, 8), 8)
            field[at, :] = field[at, :] + result[a]
        return c

    lax.fori_loop(0, EDGE, back_first, 0)

    send_faces(field, out2, inc2, 8)

    def folded(a, b):
        return jnp.sum((a * b).reshape(POINTS // EDGE, EDGE, LANES), axis=0)

    old = folded(rm[...], rm[...])
    await_faces(recv_sem.at[8], inc2)
    place_faces(field, inc2)

    image = field[...]
    mixed = folded(rm[...], image)
    square = folded(image, image)
    sums = jnp.zeros((1, LANES), F32)
    for q, value in enumerate((dots, curve, old, mixed, square)):
        one = jnp.sum(jnp.sum(value, axis=0, keepdims=True), axis=1, keepdims=True)
        sums = jnp.where(lane == q, one, sums)
    own_a[...] = sums
    rc_a[y] = sums
    send_all("gy", y, n_y, lambda t: own_a, rc_a, 5)
    await_all(recv_sem.at[5], rc_a, n_y)
    sums = jnp.sum(rc_a[...], axis=0)
    own_b[...] = sums
    rc_b[x] = sums
    send_all("gx", x, n_x, lambda t: own_b, rc_b, 6)
    await_all(recv_sem.at[6], rc_b, n_x)
    sums = jnp.sum(rc_b[...], axis=0)

    def total(q):
        return jnp.sum(jnp.where(lane == q, sums, 0.0), axis=1, keepdims=True)

    step = total(0) / total(1)
    for i in range(EDGE):
        at = pl.ds(64 * i, 64)
        sol_out[at, :] = alive * (sol_in_value(sol_in, at, loads[5], i) + step * direction[at, :])
        res_out[at, :] = rm[at, :] - step * field[at, :]
    ratio = (total(2) - 2.0 * step * total(3) + step * step * total(4)) / total(2)
    ratio_out[0] = jnp.sum(ratio)

    for phase, (landing, n) in enumerate(
        [(rc1, n_y), (rc2, n_x), (rc3, n_y), (rc4, n_y), (rc5, n_x), (rc_a, n_y), (rc_b, n_x)]
    ):
        await_all(send_sem.at[phase], landing, n)
    await_faces(send_sem.at[7], inc1)
    await_faces(send_sem.at[8], inc2)


def sol_in_value(ref, at, load, i):
    if i == 0:
        load.wait()
    return ref[at, :]


def on_device(n_x, n_y, *args):
    (
        sol,
        res,
        diag,
        cross,
        fdm,
        eig,
        vid,
        inv,
        live,
        sface,
        scode,
        pface,
        pcode,
    ) = args
    vmem = pl.BlockSpec(memory_space=pltpu.VMEM)
    smem = pl.BlockSpec(memory_space=pltpu.SMEM)
    hbm = pl.BlockSpec(memory_space=pl.ANY)
    rows1 = 64 // n_y
    field = pltpu.VMEM((POINTS, LANES), F32)
    return pl.pallas_call(
        functools.partial(kernel, n_x, n_y),
        out_shape=(
            jax.ShapeDtypeStruct((POINTS, LANES), F32),
            jax.ShapeDtypeStruct((POINTS, LANES), F32),
            jax.ShapeDtypeStruct((1,), F32),
        ),
        in_specs=[smem] + [vmem] * 6 + [hbm] * 6,
        out_specs=(vmem, vmem, smem),
        scratch_shapes=[
            field,
            field,
            pltpu.VMEM((3, POINTS, LANES), BF16),
            pltpu.VMEM((3, POINTS, LANES), BF16),
            pltpu.VMEM((3, EDGE, EDGE, LANES), F32),
            pltpu.VMEM(inv.shape, F32),
            field,
            field,
            field,
            field,
            field,
            field,
            field,
            pltpu.VMEM((LANES, 8 * LANES), BF16),
            pltpu.VMEM((LANES, 8 * LANES), BF16),
            pltpu.VMEM((64, 8 * LANES), F32),
            pltpu.VMEM((n_y, rows1, LANES), F32),
            pltpu.VMEM((n_y, rows1, LANES), F32),
            pltpu.VMEM((rows1, LANES), F32),
            pltpu.VMEM((n_x, rows1, LANES), F32),
            pltpu.VMEM((rows1, LANES), F32),
            pltpu.VMEM((n_y, rows1, LANES), F32),
            pltpu.VMEM((1, LANES), F32),
            pltpu.VMEM((n_y, 1, LANES), F32),
            pltpu.VMEM((2, LANES), F32),
            pltpu.VMEM((n_x, 2, LANES), F32),
            pltpu.VMEM((64, LANES), F32),
            pltpu.VMEM((ROWS, LANES), F32),
            pltpu.VMEM((USED, LANES), F32),
            pltpu.VMEM((ROWS, 6 * LANES), BF16),
            pltpu.VMEM((USED, 4 * LANES), BF16),
            pltpu.VMEM((LANES, 8 * LANES), BF16),
            pltpu.VMEM((LANES, 6 * LANES), BF16),
            pltpu.VMEM((ROWS, LANES), F32),
            pltpu.VMEM((ROWS, LANES), F32),
            pltpu.VMEM((ROWS, LANES), F32),
            pltpu.VMEM((ROWS, LANES), F32),
            pltpu.VMEM((USED, 8 * LANES), BF16),
            pltpu.VMEM((1, LANES), F32),
            pltpu.VMEM((n_y, 1, LANES), F32),
            pltpu.VMEM((1, LANES), F32),
            pltpu.VMEM((n_x, 1, LANES), F32),
            pltpu.SemaphoreType.DMA((6,)),
            pltpu.SemaphoreType.DMA((9,)),
            pltpu.SemaphoreType.DMA((9,)),
        ],
        compiler_params=pltpu.CompilerParams(
            collective_id=0, has_side_effects=True, vmem_limit_bytes=32 * 1024 * 1024
        ),
    )(live, vid, eig, sface, scode, pface, pcode, sol, res, diag, cross, fdm, inv)


def solution(mesh):
    both = ("gx", "gy")
    placed = (
        P(None, both),
        P(None, both),
        P(None, None, both),
        P(None, None, both),
        P(None, None, None, both),
        P(None, None, both),
        P(None, both),
        P(both, None),
        P(both),
        P(both, None, None),
        P(both, None, None),
        P(both, None, None),
        P(both, None, None),
    )
    return jax.shard_map(
        functools.partial(on_device, mesh.shape["gx"], mesh.shape["gy"]),
        mesh=mesh,
        in_specs=placed,
        out_specs=(P(None, both), P(None, both), P()),
        check_vma=False,
    )
```

time: 570 us -> 80.2 us (0.14)
  blocking collectives: 410 us -> 0 us
  local copies, waits for them, and re-layouts: 94 us -> 10.7 us
  Pallas kernels: 0 us -> 65.9 us
  other arithmetic: 34.3 us -> 0 us
  starting transfers between devices: 17 us -> 0 us
  between operations: 9.18 us -> 3.09 us
    psum x3 -> x0, blocking collectives: 310 us -> none  [the longest x1 109 us: on_device(): coarse_rhs = lax.psum(coarse_partial, ('gx', 'gy'))]
    unnamed x1 -> x0, blocking collectives: 99.5 us -> none
    pallas_call x0 -> x1, Pallas kernels: none -> 65.9 us  [on_device(): pl.pallas_call(functools.partial(kernel, n_x, n_y), out_shape=(jax.ShapeD...]
    mul x104 -> x0, local copies, waits for them, and re-layouts: 34.1 us -> none  [the longest x78 28.3 us: contract(): total = total + matrices[index][:, None, None, :] * moved[index][None]]
    gather x5 -> x0, local copies, waits for them, and re-layouts: 14.1 us -> none  [the longest x1 10.5 us: on_device(): coarse_sol[vertex_ids]]
    scatter-add x11 -> x0, other arithmetic: 12.5 us -> none  [the longest x1 5.94 us: on_device(): jax.ops.segment_sum(corners.reshape(-1), vertex_ids.reshape(-1), num_segm...]
    all_to_all x2 -> x0, starting transfers between devices: 11.8 us -> none  [face_sum(): lax.all_to_all(outgoing, 'gy', split_axis=1, concat_axis=1, tiled=True)]
    another operation x19 -> x0, local copies, waits for them, and re-layouts: 11.1 us -> none
  transfers between devices with their start and end apart: 6 -> 0, of which waited for: 0 -> 0; matrix products, arithmetic and copies ran while one was open for 12% -> 0% of each run, Pallas kernels for 0% -> 0%
where the time goes in v1:
time: 80.2 us; the launch traced here: 79.7 us
  Pallas kernels  65.9 us (82%)
  local copies, waits for them, and re-layouts  10.7 us (13%)
  between operations  3.09 us (4%)
    pallas_call x1, Pallas kernels, on_device(): pl.pallas_call(functools.partial(kernel, n_x, n_y), out_shape=(jax.ShapeD...  65.9 us
    unnamed x26, local copies, waits for them, and re-layouts  10.7 us

profile of v1, /device:TPU:1, one launch (start us, length us, event | category | flops | bytes accessed | tf_op | source)
XLA Modules:
  0.0 79.7 jit_solution(13290263162285751351)
XLA Ops:
  0.6 0.0 copy-start.10
  1.3 0.0 copy-done.10
  1.3 0.0 copy-start
  1.3 1.0 %copy-done = f32[16,8192]{1,0:T(8,128)S(1)} copy-done((f32[16,8192]{1,0:T(8,128)S(1)}, f32[16,8192]{1,0:T(8,128)}, u32[]{:S(2)}) %copy-start) | copy-done | bytes 524312
  2.4 0.0 copy-start.1
  2.4 1.0 %copy-done.1 = bf16[3,512,128]{2,1,0:T(8,128)(2,1)S(1)} copy-done((bf16[3,512,128]{2,1,0:T(8,128)(2,1)S(1)}, bf16[3,512,128]{2,1,0:T(8,128)(2,1)}, u32[]{:S(2)}) %copy-start.1) | copy-done | bytes 393240
  3.4 0.0 copy-start.2
  3.4 1.0 %copy-done.2 = bf16[3,512,128]{2,1,0:T(8,128)(2,1)S(1)} copy-done((bf16[3,512,128]{2,1,0:T(8,128)(2,1)S(1)}, bf16[3,512,128]{2,1,0:T(8,128)(2,1)}, u32[]{:S(2)}) %copy-start.2) | copy-done | bytes 393240
  4.3 0.0 copy-start.3
  4.4 0.9 %copy-done.3 = f32[512,128]{1,0:T(8,128)S(1)} copy-done((f32[512,128]{1,0:T(8,128)S(1)}, f32[512,128]{1,0:T(8,128)}, u32[]{:S(2)}) %copy-start.3) | copy-done | bytes 262168
  5.3 0.0 copy-start.4
  5.3 0.9 %copy-done.4 = f32[512,128]{1,0:T(8,128)S(1)} copy-done((f32[512,128]{1,0:T(8,128)S(1)}, f32[512,128]{1,0:T(8,128)}, u32[]{:S(2)}) %copy-start.4) | copy-done | bytes 262168
  6.3 0.0 copy-start.5
  6.3 0.9 %copy-done.5 = f32[3,8,8,128]{3,2,1,0:T(8,128)S(1)} copy-done((f32[3,8,8,128]{3,2,1,0:T(8,128)S(1)}, f32[3,8,8,128]{3,2,1,0:T(8,128)}, u32[]{:S(2)}) %copy-start.5) | copy-done | bytes 98328
  7.1 0.0 copy-start.6
  7.1 0.7 copy-done.6
  7.9 0.0 copy-start.7
  7.9 0.7 copy-done.7
  8.5 0.0 copy-start.8
  8.6 0.7 copy-done.8
  9.2 0.0 copy-start.9
  9.2 0.7 copy-done.9
  9.9 0.0 copy-start.11
  9.9 0.7 copy-done.11
  10.6 65.9 %shard_map.148 = (f32[512,128]{1,0:T(8,128)S(1)}, f32[512,128]{1,0:T(8,128)S(1)}, f32[1]{0:T(128)}) custom-call(s32[1]{0:T(128)S(6)} %copy.19.live_ref, s32[8,128]{1,0:T(8,128)S(1)} %copy-done.9, f32[3,8,128]{2,1,0:T(8,128)S(1)} %copy-done.6, s32[1,16,20]{2,1,0:T(8,128)S(1)} %copy-done.7, s32[1,16,20]{2,1,0:T(8,128)S(1)} %copy-done.8, ...), custom_call_target="tpu_custom_call" | custom-call | tf_op jit(solution)/shard_map/pallas_call | solution.py:583
  76.5 0.7 copy.20
  77.2 0.7 copy.21
Async XLA Ops:
  0.6 0.7 copy-start.10
  1.3 1.0 %copy-start = (f32[16,8192]{1,0:T(8,128)S(1)}, f32[16,8192]{1,0:T(8,128)}, u32[]{:S(2)}) copy-start(f32[16,8192]{1,0:T(8,128)} %inv_hbm.1) | copy-start | bytes 1572868
  2.4 1.0 %copy-start.1 = (bf16[3,512,128]{2,1,0:T(8,128)(2,1)S(1)}, bf16[3,512,128]{2,1,0:T(8,128)(2,1)}, u32[]{:S(2)}) copy-start(bf16[3,512,128]{2,1,0:T(8,128)(2,1)} %diag_hbm.1) | copy-start | bytes 1179652
  3.4 1.0 %copy-start.2 = (bf16[3,512,128]{2,1,0:T(8,128)(2,1)S(1)}, bf16[3,512,128]{2,1,0:T(8,128)(2,1)}, u32[]{:S(2)}) copy-start(bf16[3,512,128]{2,1,0:T(8,128)(2,1)} %cross_hbm.1) | copy-start | bytes 1179652
  4.3 0.9 %copy-start.3 = (f32[512,128]{1,0:T(8,128)S(1)}, f32[512,128]{1,0:T(8,128)}, u32[]{:S(2)}) copy-start(f32[512,128]{1,0:T(8,128)} %sol_hbm.1) | copy-start | bytes 786436
  5.3 0.9 %copy-start.4 = (f32[512,128]{1,0:T(8,128)S(1)}, f32[512,128]{1,0:T(8,128)}, u32[]{:S(2)}) copy-start(f32[512,128]{1,0:T(8,128)} %res_hbm.1) | copy-start | bytes 786436
  6.3 0.9 %copy-start.5 = (f32[3,8,8,128]{3,2,1,0:T(8,128)S(1)}, f32[3,8,8,128]{3,2,1,0:T(8,128)}, u32[]{:S(2)}) copy-start(f32[3,8,8,128]{3,2,1,0:T(8,128)} %fdm_hbm.1) | copy-start | bytes 294916
  7.1 0.7 copy-start.6
  7.9 0.7 copy-start.7
  8.5 0.7 copy-start.8
  9.2 0.7 copy-start.9
  9.9 0.7 copy-start.11

commit v2 on v1

--- a/solution.py
+++ b/solution.py
@@ -81,6 +81,22 @@
 def kernel(
     n_x,
     n_y,
+    sol_hbm,
+    res_hbm,
+    diag_hbm,
+    cross_hbm,
+    fdm_hbm,
+    eig_hbm,
+    vid_hbm,
+    inv_hbm,
+    live_hbm,
+    sface_hbm,
+    scode_hbm,
+    pface_hbm,
+    pcode_hbm,
+    sol_out,
+    res_out,
+    ratio_out,
     live_ref,
     vid_ref,
     eig_ref,
@@ -88,21 +104,13 @@
     scode_ref,
     pface_ref,
     pcode_ref,
-    sol_hbm,
-    res_hbm,
-    diag_hbm,
-    cross_hbm,
-    fdm_hbm,
-    inv_hbm,
-    sol_out,
-    res_out,
-    ratio_out,
     sol_in,
     rm,
     diag,
     cross,
     fdm,
-    inv,
+    block,
+    blocks,
     buf_a,
     buf_b,
     field,
@@ -121,8 +129,6 @@
     rc3,
     own4,
     rc4,
-    own5,
-    rc5,
     coarse,
     idm,
     cdm,
@@ -140,53 +146,78 @@
     own_b,
     rc_b,
     in_sem,
+    out_sem,
     send_sem,
     recv_sem,
 ):
     x, y = lax.axis_index("gx"), lax.axis_index("gy")
+    z, core = x // 2, lax.rem(x, 2)
+    n_z, n_p = n_x // 2, 2 * n_y
+    me = core * n_y + y
     offsets = (1, n_y - 1, 2, n_y - 2, n_y // 2)
     back_to = (1, 0, 3, 2, 4)
 
-    loads = [
-        pltpu.make_async_copy(s, d, in_sem.at[i])
-        for i, (s, d) in enumerate(
-            [(res_hbm, rm), (fdm_hbm, fdm), (inv_hbm, inv), (diag_hbm, diag), (cross_hbm, cross), (sol_hbm, sol_in)]
-        )
-    ]
-    for load in loads:
+    moved = dict(
+        live=(live_hbm, live_ref),
+        residual=(res_hbm, rm),
+        vid=(vid_hbm, vid_ref),
+        sface=(sface_hbm, sface_ref),
+        scode=(scode_hbm, scode_ref),
+        pface=(pface_hbm, pface_ref),
+        pcode=(pcode_hbm, pcode_ref),
+        fdm=(fdm_hbm, fdm),
+        eig=(eig_hbm, eig_ref),
+        diag=(diag_hbm, diag),
+        cross=(cross_hbm, cross),
+        sol=(sol_hbm, sol_in),
+    )
+    loads = {n: pltpu.make_async_copy(s, d, in_sem.at[i]) for i, (n, (s, d)) in enumerate(moved.items())}
+    for load in loads.values():
         load.start()
 
     barrier = pltpu.get_barrier_semaphore()
 
-    def greet(axis, me, n):
+    def in_plane(t):
+        return (2 * z + t // n_y, lax.rem(t, n_y))
+
+    def in_line(t):
+        return (2 * t + core, y)
+
+    def greet(where, own, n):
         def body(k, c):
-            pl.semaphore_signal(barrier, inc=1, device_id={axis: lax.rem(me + k, n)}, device_id_type=MESH)
+            pl.semaphore_signal(barrier, inc=1, device_id=where(lax.rem(own + k, n)), device_id_type=MESH)
             return c
 
         lax.fori_loop(1, n, body, 0)
 
-    greet("gy", y, n_y)
-    greet("gx", x, n_x)
-
-    def send_all(axis, me, n, source, landing, phase):
+    greet(in_plane, me, n_p)
+    greet(in_line, z, n_z)
+    beside = lax.rem(x + n_x - 1 + 2 * core, n_x)
+    pl.semaphore_signal(barrier, inc=1, device_id=(beside, y), device_id_type=MESH)
+
+    sent = []
+
+    def send_all(where, own, n, source, landing, phase):
         def body(k, c):
-            target = lax.rem(me + k, n)
+            target = lax.rem(own + k, n)
             pltpu.make_async_remote_copy(
                 src_ref=source(target),
-                dst_ref=landing.at[me],
+                dst_ref=landing.at[own],
                 send_sem=send_sem.at[phase],
                 recv_sem=recv_sem.at[phase],
-                device_id={axis: target},
+                device_id=where(target),
                 device_id_type=MESH,
             ).start()
             return c
 
         lax.fori_loop(1, n, body, 0)
-
-    def await_all(sem, landing, n):
+        sent.append((phase, landing.at[pl.ds(0, n - 1)]))
+
+    def await_all(phase, landing, n):
         some = landing.at[pl.ds(0, n - 1)]
-        pltpu.make_async_copy(some, some, sem).wait()
-
+        pltpu.make_async_copy(some, some, recv_sem.at[phase]).wait()
+
+    loads["live"].wait()
     alive = (iota((1, LANES), 1) < live_ref[0]).astype(F32)
     lane = iota((1, LANES), 1)
     sub8 = iota((EDGE, 1), 0)
@@ -199,7 +230,8 @@
 
     inc1[pl.ds(SPARE, 8), :] = jnp.zeros((8, LANES), F32)
     inc2[pl.ds(SPARE, 8), :] = jnp.zeros((8, LANES), F32)
-    loads[0].wait()
+    loads["residual"].wait()
+    loads["vid"].wait()
     along_i = [None, None]
     for i in range(EDGE):
         slab = rm[pl.ds(64 * i, 64), :] * alive
@@ -227,14 +259,16 @@
                 y_one[:, at] = (low_iota == (ids & 127)).astype(F32).astype(BF16)
     both = lax.dot_general(x_one[...], y_one[...], NT, preferred_element_type=F32)
     partial = both[0:64] + both[64:128]
-    rows1 = 64 // n_y
-    for q in range(n_y):
-        part[q] = partial[rows1 * q : rows1 * q + rows1]
-
-    pl.semaphore_wait(barrier, n_x + n_y - 2)
-
-    send_all("gy", y, n_y, lambda t: part.at[t], rc1, 0)
-    rc1[y] = part[y]
+    for q in range(n_p):
+        part[q] = partial[2 * q : 2 * q + 2]
+
+    pl.semaphore_wait(barrier, n_p + n_z - 1)
+
+    send_all(in_plane, me, n_p, lambda t: part.at[t], rc1, 0)
+    rc1[me] = part[me]
+    send_all(in_plane, me, n_p, lambda t: inv_hbm.at[:, pl.ds(pl.multiple_of(256 * t, 256), 256)], block, 9)
+    keep = pltpu.make_async_copy(inv_hbm.at[:, pl.ds(pl.multiple_of(256 * me, 256), 256)], block.at[me], in_sem.at[12])
+    keep.start()
 
     def column(row, rows, swap=0):
         width = row.shape[1]
@@ -242,6 +276,8 @@
         kept = jnp.where(diagonal, row.astype(F32) + 1.0, 0.0)
         return jnp.broadcast_to(jnp.sum(kept, axis=1, keepdims=True) - 1.0, (rows, LANES))
 
+    for name in ("sface", "scode", "pface", "pcode"):
+        loads[name].wait()
     idm[pl.ds(0, 32), :] = column(sface_ref[0, pl.ds(y, 1), :], 32, 1)
     idm[pl.ds(32, 32), :] = column(sface_ref[0, pl.ds(y, 1), :], 32)
     cdm[pl.ds(0, 32), :] = column(scode_ref[0, pl.ds(y, 1), :], 32)
@@ -274,11 +310,11 @@
         fits = (source == (grid_lane & 63)) & ((grid_row < 64) if t < 4 else (grid_row >= 64))
         perm[:, pl.ds(t * LANES, LANES)] = fits.astype(F32).astype(BF16)
 
-    await_all(recv_sem.at[0], rc1, n_y)
+    await_all(0, rc1, n_p)
     mine = jnp.sum(rc1[...], axis=0)
     own2[...] = mine
-    rc2[x] = mine
-    send_all("gx", x, n_x, lambda t: own2, rc2, 1)
+    rc2[z] = mine
+    send_all(in_line, z, n_z, lambda t: own2, rc2, 1)
 
     def sum_of(coef, slabs, a):
         total = coef(0, a) * slabs(0)
@@ -312,7 +348,8 @@
     def put_j(ref, a, value):
         ref.reshape(EDGE, EDGE, EDGE, LANES)[:, pl.ds(a, 1)] = value.reshape(EDGE, 1, EDGE, LANES)
 
-    loads[1].wait()
+    loads["fdm"].wait()
+    loads["eig"].wait()
     per_row(lambda a: put_i(buf_a, a, sum_of(forward(0), slab_i(rm), a)))
     per_row(lambda a: put_j(buf_b, a, sum_of(forward(1), slab_j(buf_a), a)))
     for k in range(EDGE):
@@ -325,12 +362,6 @@
         put_i(buf_b, a, value / (buf_a[pl.ds(0, 64), :] + eig_ref[2, pl.ds(a, 1), :]))
 
     per_row(spectral)
-
-    await_all(recv_sem.at[1], rc2, n_x)
-    mine = jnp.sum(rc2[...], axis=0)
-    own3[...] = mine
-    rc3[y] = mine
-    send_all("gy", y, n_y, lambda t: own3, rc3, 2)
 
     per_row(lambda a: put_i(turned, a, sum_of(backward(2), slab_i(buf_b), a)))
     for k in range(EDGE):
@@ -375,10 +406,11 @@
                 device_id=target,
                 device_id_type=MESH,
             ).start()
-
-    def await_faces(sem, inc):
+        sent.append((phase, inc.at[pl.ds(0, SENT_ROWS)]))
+
+    def await_faces(phase, inc):
         some = inc.at[pl.ds(0, SENT_ROWS)]
-        pltpu.make_async_copy(some, some, sem).wait()
+        pltpu.make_async_copy(some, some, recv_sem.at[phase]).wait()
 
     def place_faces(ref, inc):
         high, low = split(inc[pl.ds(FIRST, USED), :])
@@ -400,38 +432,40 @@
                 at = pl.ds(7 * (f - 4), 64, stride=EDGE)
                 ref[at, :] = ref[at, :] + more
 
+    await_all(9, block, n_p)
+    keep.wait()
+    for n in range(n_p):
+        high, low = split(block[n])
+        blocks[16 * n : 16 * n + 16, :] = high
+        blocks[16 * (n_p + n) : 16 * (n_p + n) + 16, :] = low
+
+    await_all(1, rc2, n_z)
+    mine = jnp.sum(rc2[...], axis=0)
+    high, low = split(jnp.concatenate([mine[0:1], mine[1:2]], axis=1))
+    pair = jnp.concatenate([high.astype(F32), low.astype(F32), jnp.zeros((14, 2 * LANES), F32)], axis=0).astype(BF16)
+    product = lax.dot_general(pair, blocks[...], NT, preferred_element_type=F32)
+    count = 16 * n_p
+    product = product[0:1, :count] + (product[1:2, :count] + product[0:1, count:])
+    mine = jnp.concatenate([product[:, LANES * h : LANES * h + LANES] for h in range(4)], axis=0)
+    own3[...] = mine
+    rc3[me] = mine
+    send_all(in_plane, me, n_p, lambda t: own3, rc3, 2)
+
     send_faces(field, out1, inc1, 7)
 
-    await_all(recv_sem.at[2], rc3, n_y)
-    loads[2].wait()
-
-    def rows_times(q, acc):
-        for r in range(rows1):
-            at = pl.ds(pl.multiple_of((q * rows1 + r) * LANES, LANES), LANES)
-            acc = acc + inv[:, at] * rc3[q, r : r + 1, :]
-        return acc
-
-    acc = lax.fori_loop(0, n_y, rows_times, jnp.zeros((16, LANES), F32))
-    own_values = jnp.sum(acc, axis=1, keepdims=True)
-    spot = iota((16, LANES), 1) == 16 * lax.rem(y, 8) + iota((16, LANES), 0)
-    row = jnp.sum(jnp.where(spot, own_values, 0.0), axis=0, keepdims=True)
-    own4[...] = row
-    rc4[y] = row
-
-    send_all("gy", y, n_y, lambda t: own4, rc4, 3)
-    await_faces(recv_sem.at[7], inc1)
+    await_all(2, rc3, n_p)
+    mine = jnp.sum(rc3[...], axis=0)
+    own4[...] = mine
+    rc4[z] = mine
+    send_all(in_line, z, n_z, lambda t: own4, rc4, 3)
+    await_faces(7, inc1)
     place_faces(field, inc1)
-
-    await_all(recv_sem.at[3], rc4, n_y)
-    pair = jnp.concatenate([jnp.sum(rc4[0:8], axis=0), jnp.sum(rc4[8:16], axis=0)], axis=0)
-    own5[...] = pair
-    rc5[x] = pair
-    send_all("gx", x, n_x, lambda t: own5, rc5, 4)
-    loads[3].wait()
-    loads[4].wait()
-    await_all(recv_sem.at[4], rc5, n_x)
-    for q in range(n_x):
-        coarse[pl.ds(2 * q, 2), :] = rc5[q]
+    loads["diag"].wait()
+    loads["cross"].wait()
+
+    await_all(3, rc4, n_z)
+    for q in range(n_z):
+        coarse[pl.ds(4 * q, 4), :] = rc4[q]
 
     high, low = split(coarse[...])
     at_low = jnp.dot(jnp.concatenate([high, low], axis=0), y_one[...], preferred_element_type=F32)
@@ -513,7 +547,7 @@
         return jnp.sum((a * b).reshape(POINTS // EDGE, EDGE, LANES), axis=0)
 
     old = folded(rm[...], rm[...])
-    await_faces(recv_sem.at[8], inc2)
+    await_faces(8, inc2)
     place_faces(field, inc2)
 
     image = field[...]
@@ -524,61 +558,46 @@
         one = jnp.sum(jnp.sum(value, axis=0, keepdims=True), axis=1, keepdims=True)
         sums = jnp.where(lane == q, one, sums)
     own_a[...] = sums
-    rc_a[y] = sums
-    send_all("gy", y, n_y, lambda t: own_a, rc_a, 5)
-    await_all(recv_sem.at[5], rc_a, n_y)
+    rc_a[me] = sums
+    send_all(in_plane, me, n_p, lambda t: own_a, rc_a, 5)
+    await_all(5, rc_a, n_p)
     sums = jnp.sum(rc_a[...], axis=0)
     own_b[...] = sums
-    rc_b[x] = sums
-    send_all("gx", x, n_x, lambda t: own_b, rc_b, 6)
-    await_all(recv_sem.at[6], rc_b, n_x)
+    rc_b[z] = sums
+    send_all(in_line, z, n_z, lambda t: own_b, rc_b, 6)
+    await_all(6, rc_b, n_z)
     sums = jnp.sum(rc_b[...], axis=0)
 
     def total(q):
         return jnp.sum(jnp.where(lane == q, sums, 0.0), axis=1, keepdims=True)
 
     step = total(0) / total(1)
+    stores = []
+    loads["sol"].wait()
     for i in range(EDGE):
         at = pl.ds(64 * i, 64)
-        sol_out[at, :] = alive * (sol_in_value(sol_in, at, loads[5], i) + step * direction[at, :])
-        res_out[at, :] = rm[at, :] - step * field[at, :]
+        sol_in[at, :] = alive * (sol_in[at, :] + step * direction[at, :])
+        rm[at, :] = rm[at, :] - step * field[at, :]
+        if i % 4 == 3:
+            at = pl.ds(64 * (i - 3), 256)
+            for q, (source, target) in enumerate(((sol_in, sol_out), (rm, res_out))):
+                store = pltpu.make_async_copy(source.at[at], target.at[at], out_sem.at[q, i // 4])
+                store.start()
+                stores.append(store)
     ratio = (total(2) - 2.0 * step * total(3) + step * step * total(4)) / total(2)
     ratio_out[0] = jnp.sum(ratio)
 
-    for phase, (landing, n) in enumerate(
-        [(rc1, n_y), (rc2, n_x), (rc3, n_y), (rc4, n_y), (rc5, n_x), (rc_a, n_y), (rc_b, n_x)]
-    ):
-        await_all(send_sem.at[phase], landing, n)
-    await_faces(send_sem.at[7], inc1)
-    await_faces(send_sem.at[8], inc2)
-
-
-def sol_in_value(ref, at, load, i):
-    if i == 0:
-        load.wait()
-    return ref[at, :]
+    for phase, some in sent:
+        pltpu.make_async_copy(some, some, send_sem.at[phase]).wait()
+    for store in stores:
+        store.wait()
 
 
 def on_device(n_x, n_y, *args):
-    (
-        sol,
-        res,
-        diag,
-        cross,
-        fdm,
-        eig,
-        vid,
-        inv,
-        live,
-        sface,
-        scode,
-        pface,
-        pcode,
-    ) = args
-    vmem = pl.BlockSpec(memory_space=pltpu.VMEM)
+    live, vid, eig, sface, scode, pface, pcode = (args[i] for i in (8, 6, 5, 9, 10, 11, 12))
     smem = pl.BlockSpec(memory_space=pltpu.SMEM)
     hbm = pl.BlockSpec(memory_space=pl.ANY)
-    rows1 = 64 // n_y
+    n_p, n_z = 2 * n_y, n_x // 2
     field = pltpu.VMEM((POINTS, LANES), F32)
     return pl.pallas_call(
         functools.partial(kernel, n_x, n_y),
@@ -587,15 +606,23 @@
             jax.ShapeDtypeStruct((POINTS, LANES), F32),
             jax.ShapeDtypeStruct((1,), F32),
         ),
-        in_specs=[smem] + [vmem] * 6 + [hbm] * 6,
-        out_specs=(vmem, vmem, smem),
+        in_specs=[hbm] * len(args),
+        out_specs=(hbm, hbm, smem),
         scratch_shapes=[
+            pltpu.SMEM((1,), jnp.int32),
+            pltpu.VMEM(vid.shape, jnp.int32),
+            pltpu.VMEM(eig.shape, F32),
+            pltpu.VMEM(sface.shape, jnp.int32),
+            pltpu.VMEM(scode.shape, jnp.int32),
+            pltpu.VMEM(pface.shape, jnp.int32),
+            pltpu.VMEM(pcode.shape, jnp.int32),
             field,
             field,
             pltpu.VMEM((3, POINTS, LANES), BF16),
             pltpu.VMEM((3, POINTS, LANES), BF16),
             pltpu.VMEM((3, EDGE, EDGE, LANES), F32),
-            pltpu.VMEM(inv.shape, F32),
+            pltpu.VMEM((n_p, 16, 2 * LANES), F32),
+            pltpu.VMEM((32 * n_p, 2 * LANES), BF16),
             field,
             field,
             field,
@@ -606,16 +633,14 @@
             pltpu.VMEM((LANES, 8 * LANES), BF16),
             pltpu.VMEM((LANES, 8 * LANES), BF16),
             pltpu.VMEM((64, 8 * LANES), F32),
-            pltpu.VMEM((n_y, rows1, LANES), F32),
-            pltpu.VMEM((n_y, rows1, LANES), F32),
-            pltpu.VMEM((rows1, LANES), F32),
-            pltpu.VMEM((n_x, rows1, LANES), F32),
-            pltpu.VMEM((rows1, LANES), F32),
-            pltpu.VMEM((n_y, rows1, LANES), F32),
-            pltpu.VMEM((1, LANES), F32),
-            pltpu.VMEM((n_y, 1, LANES), F32),
+            pltpu.VMEM((n_p, 2, LANES), F32),
+            pltpu.VMEM((n_p, 2, LANES), F32),
             pltpu.VMEM((2, LANES), F32),
-            pltpu.VMEM((n_x, 2, LANES), F32),
+            pltpu.VMEM((n_z, 2, LANES), F32),
+            pltpu.VMEM((4, LANES), F32),
+            pltpu.VMEM((n_p, 4, LANES), F32),
+            pltpu.VMEM((4, LANES), F32),
+            pltpu.VMEM((n_z, 4, LANES), F32),
             pltpu.VMEM((64, LANES), F32),
             pltpu.VMEM((ROWS, LANES), F32),
             pltpu.VMEM((USED, LANES), F32),
@@ -629,17 +654,18 @@
             pltpu.VMEM((ROWS, LANES), F32),
             pltpu.VMEM((USED, 8 * LANES), BF16),
             pltpu.VMEM((1, LANES), F32),
-            pltpu.VMEM((n_y, 1, LANES), F32),
+            pltpu.VMEM((n_p, 1, LANES), F32),
             pltpu.VMEM((1, LANES), F32),
-            pltpu.VMEM((n_x, 1, LANES), F32),
-            pltpu.SemaphoreType.DMA((6,)),
-            pltpu.SemaphoreType.DMA((9,)),
-            pltpu.SemaphoreType.DMA((9,)),
+            pltpu.VMEM((n_z, 1, LANES), F32),
+            pltpu.SemaphoreType.DMA((13,)),
+            pltpu.SemaphoreType.DMA((2, 2)),
+            pltpu.SemaphoreType.DMA((10,)),
+            pltpu.SemaphoreType.DMA((10,)),
         ],
         compiler_params=pltpu.CompilerParams(
-            collective_id=0, has_side_effects=True, vmem_limit_bytes=32 * 1024 * 1024
+            collective_id=0, has_side_effects=True, vmem_limit_bytes=60 * 1024 * 1024
         ),
-    )(live, vid, eig, sface, scode, pface, pcode, sol, res, diag, cross, fdm, inv)
+    )(*args)
 
 
 def solution(mesh):

time: 80.2 us -> 66.6 us (0.83)
  local copies, waits for them, and re-layouts: 10.7 us -> 2.42 us
  Pallas kernels: 65.9 us -> 61 us
    unnamed x26 -> x4, local copies, waits for them, and re-layouts: 10.7 us -> 2.42 us
    pallas_call x1, Pallas kernels: 65.9 us -> 61 us  [on_device(): pl.pallas_call(functools.partial(kernel, n_x, n_y), out_shape=(jax.ShapeD...]
where the time goes in v2:
time: 66.6 us; the launch traced here: 66.5 us
  Pallas kernels  61 us (92%)
  between operations  3.06 us (5%)
  local copies, waits for them, and re-layouts  2.42 us (4%)
    pallas_call x1, Pallas kernels, on_device(): pl.pallas_call(functools.partial(kernel, n_x, n_y), out_shape=(jax.ShapeD...  61 us
    unnamed x4, local copies, waits for them, and re-layouts  2.42 us

profile of v2, /device:TPU:1, one launch (start us, length us, event | category | flops | bytes accessed | tf_op | source)
XLA Modules:
  0.0 66.5 jit_solution(6119573285216505797)
XLA Ops:
  1.3 61.0 %shard_map.148 = (f32[512,128]{1,0:T(8,128)}, f32[512,128]{1,0:T(8,128)}, f32[1]{0:T(128)}) custom-call(f32[512,128]{1,0:T(8,128)} %sol_hbm.1, f32[512,128]{1,0:T(8,128)} %res_hbm.1, bf16[3,512,128]{2,1,0:T(8,128)(2,1)} %diag_hbm.1, bf16[3,512,128]{2,1,0:T(8,128)(2,1)} %cross_hbm.1, f32[3,8,8,128]{3,2,1,0:T(8,128)} %fdm_hbm.1, f32[3,8,128]{2,1,0:T(8,128)} %eig_hbm.1, ...), custom_call_target="tpu_custom_call" | custom-call | tf_op jit(solution)/shard_map/pallas_call | solution.py:602
  62.3 0.0 copy-start
  62.3 1.7 %copy.20 = f32[512,128]{1,0:T(8,128)} copy(f32[512,128]{1,0:T(8,128)} %get-tuple-element.6) | data formatting | bytes 524288
  64.0 0.0 copy-done
  64.0 0.7 %copy.21 = f32[512,128]{1,0:T(8,128)} copy(f32[512,128]{1,0:T(8,128)S(1)} %copy-done) | data formatting | bytes 524288
Async XLA Ops:
  62.3 1.7 %copy-start = (f32[512,128]{1,0:T(8,128)S(1)}, f32[512,128]{1,0:T(8,128)}, u32[]{:S(2)}) copy-start(f32[512,128]{1,0:T(8,128)} %get-tuple-element.7) | copy-start | bytes 786436

commit v3 on v2

--- a/solution.py
+++ b/solution.py
@@ -81,7 +81,6 @@
 def kernel(
     n_x,
     n_y,
-    sol_hbm,
     res_hbm,
     diag_hbm,
     cross_hbm,
@@ -94,9 +93,9 @@
     scode_hbm,
     pface_hbm,
     pcode_hbm,
-    sol_out,
-    res_out,
-    ratio_out,
+    direction_out,
+    image_out,
+    sums_out,
     live_ref,
     vid_ref,
     eig_ref,
@@ -104,7 +103,6 @@
     scode_ref,
     pface_ref,
     pcode_ref,
-    sol_in,
     rm,
     diag,
     cross,
@@ -145,6 +143,8 @@
     rc_a,
     own_b,
     rc_b,
+    totals,
+    ready,
     in_sem,
     out_sem,
     send_sem,
@@ -169,7 +169,6 @@
         eig=(eig_hbm, eig_ref),
         diag=(diag_hbm, diag),
         cross=(cross_hbm, cross),
-        sol=(sol_hbm, sol_in),
     )
     loads = {n: pltpu.make_async_copy(s, d, in_sem.at[i]) for i, (n, (s, d)) in enumerate(moved.items())}
     for load in loads.values():
@@ -177,41 +176,62 @@
 
     barrier = pltpu.get_barrier_semaphore()
 
-    def in_plane(t):
-        return (2 * z + t // n_y, lax.rem(t, n_y))
-
-    def in_line(t):
-        return (2 * t + core, y)
-
-    def greet(where, own, n):
+    def at_plane(k):
+        k = k + k // 10
+        a, b = y // 4 + 2 + k // 4, y + 2 + k
+        return 4 * lax.rem(a, 4) + lax.rem(b, 4)
+
+    def over_plane(act):
         def body(k, c):
-            pl.semaphore_signal(barrier, inc=1, device_id=where(lax.rem(own + k, n)), device_id_type=MESH)
+            other = at_plane(k)
+            for half in range(2):
+                act(2 * z + half, other, half * n_y + other)
             return c
 
-        lax.fori_loop(1, n, body, 0)
-
-    greet(in_plane, me, n_p)
-    greet(in_line, z, n_z)
-    beside = lax.rem(x + n_x - 1 + 2 * core, n_x)
-    pl.semaphore_signal(barrier, inc=1, device_id=(beside, y), device_id_type=MESH)
+        lax.fori_loop(0, n_y - 1, body, 0)
+        act(2 * z + 1 - core, y, (1 - core) * n_y + y)
+
+    def over_line(act):
+        def body(k, c):
+            away = (k + 1) // 2
+            act(lax.rem(z + n_z + n_z // 2 + away * (1 - 2 * lax.rem(k, 2)), n_z))
+            return c
+
+        lax.fori_loop(0, n_z - 1, body, 0)
+
+    def at_device(i, j):
+        return dict(device_id=(i, j), device_id_type=MESH)
+
+    def greet_plane(k, c):
+        pl.semaphore_signal(barrier, inc=1, **at_device(2 * z, at_plane(k)))
+        return c
+
+    lax.fori_loop(0, n_y - 1, greet_plane, 0)
+
+    @pl.when(core == 1)
+    def _():
+        pl.semaphore_signal(barrier, inc=1, **at_device(2 * z, y))
+
+    over_line(lambda t: pl.semaphore_signal(barrier, inc=1, **at_device(2 * t + 1, y)))
 
     sent = []
 
-    def send_all(where, own, n, source, landing, phase):
-        def body(k, c):
-            target = lax.rem(own + k, n)
-            pltpu.make_async_remote_copy(
-                src_ref=source(target),
-                dst_ref=landing.at[own],
-                send_sem=send_sem.at[phase],
-                recv_sem=recv_sem.at[phase],
-                device_id=where(target),
-                device_id_type=MESH,
-            ).start()
-            return c
-
-        lax.fori_loop(1, n, body, 0)
-        sent.append((phase, landing.at[pl.ds(0, n - 1)]))
+    def send(source, target, phase, i, j):
+        pltpu.make_async_remote_copy(
+            src_ref=source,
+            dst_ref=target,
+            send_sem=send_sem.at[phase],
+            recv_sem=recv_sem.at[phase],
+            **at_device(i, j),
+        ).start()
+
+    def send_plane(source, landing, phase):
+        over_plane(lambda i, j, t: send(source(t), landing.at[me], phase, i, j))
+        sent.append((phase, landing.at[pl.ds(0, n_p - 1)]))
+
+    def send_line(source, landing, phase):
+        over_line(lambda t: send(source, landing.at[z], phase, 2 * t + core, y))
+        sent.append((phase, landing.at[pl.ds(0, n_z - 1)]))
 
     def await_all(phase, landing, n):
         some = landing.at[pl.ds(0, n - 1)]
@@ -262,11 +282,18 @@
     for q in range(n_p):
         part[q] = partial[2 * q : 2 * q + 2]
 
-    pl.semaphore_wait(barrier, n_p + n_z - 1)
-
-    send_all(in_plane, me, n_p, lambda t: part.at[t], rc1, 0)
+    @pl.when(core == 0)
+    def _():
+        pl.semaphore_wait(barrier, n_p - 1)
+        pl.semaphore_signal(ready, inc=1, **at_device(2 * z + 1, y))
+
+    @pl.when(core == 1)
+    def _():
+        pl.semaphore_wait(ready, 1)
+
+    send_plane(lambda t: part.at[t], rc1, 0)
     rc1[me] = part[me]
-    send_all(in_plane, me, n_p, lambda t: inv_hbm.at[:, pl.ds(pl.multiple_of(256 * t, 256), 256)], block, 9)
+    send_plane(lambda t: inv_hbm.at[:, pl.ds(pl.multiple_of(256 * t, 256), 256)], block, 9)
     keep = pltpu.make_async_copy(inv_hbm.at[:, pl.ds(pl.multiple_of(256 * me, 256), 256)], block.at[me], in_sem.at[12])
     keep.start()
 
@@ -314,7 +341,17 @@
     mine = jnp.sum(rc1[...], axis=0)
     own2[...] = mine
     rc2[z] = mine
-    send_all(in_line, z, n_z, lambda t: own2, rc2, 1)
+
+    @pl.when(core == 1)
+    def _():
+        pl.semaphore_wait(barrier, 2 * (n_z - 1))
+        pl.semaphore_signal(ready, inc=1, **at_device(2 * z, y))
+
+    @pl.when(core == 0)
+    def _():
+        pl.semaphore_wait(ready, 1)
+
+    send_line(own2, rc2, 1)
 
     def sum_of(coef, slabs, a):
         total = coef(0, a) * slabs(0)
@@ -386,26 +423,19 @@
         out[...] = found
         inc[pl.ds(FIRST, 32), :] = found[0:32]
         hops = [
-            (PEER_ROW + PEER_ROWS * g, PEER_ROW + PEER_ROWS * back_to[g], PEER_ROWS, {"gy": lax.rem(y + offsets[g], n_y)})
+            (PEER_ROW + PEER_ROWS * g, PEER_ROW + PEER_ROWS * back_to[g], PEER_ROWS, (x, lax.rem(y + offsets[g], n_y)))
             for g in range(5)
         ] + [
             (
                 PIPE_ROW + PIPE_ROWS * s,
                 PIPE_ROW + PIPE_ROWS * (1 - s),
                 PIPE_ROWS,
-                {"gx": lax.rem(x + n_x - 1 + 2 * s, n_x)},
+                (lax.rem(x + n_x - 1 + 2 * s, n_x), y),
             )
             for s in range(2)
         ]
         for start, land, count, target in hops:
-            pltpu.make_async_remote_copy(
-                src_ref=out.at[pl.ds(start, count)],
-                dst_ref=inc.at[pl.ds(land, count)],
-                send_sem=send_sem.at[phase],
-                recv_sem=recv_sem.at[phase],
-                device_id=target,
-                device_id_type=MESH,
-            ).start()
+            send(out.at[pl.ds(start, count)], inc.at[pl.ds(land, count)], phase, *target)
         sent.append((phase, inc.at[pl.ds(0, SENT_ROWS)]))
 
     def await_faces(phase, inc):
@@ -449,7 +479,7 @@
     mine = jnp.concatenate([product[:, LANES * h : LANES * h + LANES] for h in range(4)], axis=0)
     own3[...] = mine
     rc3[me] = mine
-    send_all(in_plane, me, n_p, lambda t: own3, rc3, 2)
+    send_plane(lambda t: own3, rc3, 2)
 
     send_faces(field, out1, inc1, 7)
 
@@ -457,7 +487,7 @@
     mine = jnp.sum(rc3[...], axis=0)
     own4[...] = mine
     rc4[z] = mine
-    send_all(in_line, z, n_z, lambda t: own4, rc4, 3)
+    send_line(own4, rc4, 3)
     await_faces(7, inc1)
     place_faces(field, inc1)
     loads["diag"].wait()
@@ -485,6 +515,9 @@
         at = pl.ds(64 * i, 64)
         lifted = float(HATS[0, i]) * planes[0] + float(HATS[1, i]) * planes[1]
         direction[at, :] = alive * (field[at, :] + lifted)
+
+    stores = [pltpu.make_async_copy(direction, direction_out, out_sem.at[0])]
+    stores[0].start()
 
     def take(ref, start, stride):
         return [ref[pl.ds(pl.multiple_of(start + stride * m, 8), 8), :] for m in range(EDGE)]
@@ -550,6 +583,8 @@
     await_faces(8, inc2)
     place_faces(field, inc2)
 
+    stores.append(pltpu.make_async_copy(field, image_out, out_sem.at[1]))
+    stores[1].start()
     image = field[...]
     mixed = folded(rm[...], image)
     square = folded(image, image)
@@ -559,36 +594,80 @@
         sums = jnp.where(lane == q, one, sums)
     own_a[...] = sums
     rc_a[me] = sums
-    send_all(in_plane, me, n_p, lambda t: own_a, rc_a, 5)
+    send_plane(lambda t: own_a, rc_a, 5)
     await_all(5, rc_a, n_p)
     sums = jnp.sum(rc_a[...], axis=0)
     own_b[...] = sums
     rc_b[z] = sums
-    send_all(in_line, z, n_z, lambda t: own_b, rc_b, 6)
+    send_line(own_b, rc_b, 6)
     await_all(6, rc_b, n_z)
     sums = jnp.sum(rc_b[...], axis=0)
 
+    totals[...] = sums
+    stores.append(pltpu.make_async_copy(totals, sums_out, out_sem.at[2]))
+    stores[2].start()
+    for phase, some in sent:
+        pltpu.make_async_copy(some, some, send_sem.at[phase]).wait()
+    for store in stores:
+        store.wait()
+
+
+def update(
+    sol_hbm,
+    res_hbm,
+    direction_hbm,
+    image_hbm,
+    sums_hbm,
+    live_hbm,
+    sol_out,
+    res_out,
+    ratio_out,
+    sol,
+    res,
+    direction,
+    image,
+    sums_ref,
+    live_ref,
+    in_sem,
+    small_sem,
+    out_sem,
+):
+    small = [
+        pltpu.make_async_copy(s, d, small_sem.at[i]) for i, (s, d) in enumerate(((sums_hbm, sums_ref), (live_hbm, live_ref)))
+    ]
+    for copy in small:
+        copy.start()
+    half = POINTS // 2
+    loads = []
+    for h in range(2):
+        at = pl.ds(half * h, half)
+        for q, (s, d) in enumerate(((sol_hbm, sol), (direction_hbm, direction), (res_hbm, res), (image_hbm, image))):
+            loads.append(pltpu.make_async_copy(s.at[at], d.at[at], in_sem.at[h, q]))
+    for copy in loads:
+        copy.start()
+    for copy in small:
+        copy.wait()
+    lane = iota((1, LANES), 1)
+    sums = sums_ref[...]
+
     def total(q):
         return jnp.sum(jnp.where(lane == q, sums, 0.0), axis=1, keepdims=True)
 
     step = total(0) / total(1)
+    alive = (lane < live_ref[0]).astype(F32)
     stores = []
-    loads["sol"].wait()
-    for i in range(EDGE):
-        at = pl.ds(64 * i, 64)
-        sol_in[at, :] = alive * (sol_in[at, :] + step * direction[at, :])
-        rm[at, :] = rm[at, :] - step * field[at, :]
-        if i % 4 == 3:
-            at = pl.ds(64 * (i - 3), 256)
-            for q, (source, target) in enumerate(((sol_in, sol_out), (rm, res_out))):
-                store = pltpu.make_async_copy(source.at[at], target.at[at], out_sem.at[q, i // 4])
-                store.start()
-                stores.append(store)
+    for h in range(2):
+        at = pl.ds(half * h, half)
+        for copy in loads[4 * h : 4 * h + 4]:
+            copy.wait()
+        sol[at, :] = alive * (sol[at, :] + step * direction[at, :])
+        res[at, :] = res[at, :] * alive - step * image[at, :]
+        for q, (s, d) in enumerate(((sol, sol_out), (res, res_out))):
+            store = pltpu.make_async_copy(s.at[at], d.at[at], out_sem.at[h, q])
+            store.start()
+            stores.append(store)
     ratio = (total(2) - 2.0 * step * total(3) + step * step * total(4)) / total(2)
     ratio_out[0] = jnp.sum(ratio)
-
-    for phase, some in sent:
-        pltpu.make_async_copy(some, some, send_sem.at[phase]).wait()
     for store in stores:
         store.wait()
 
@@ -599,15 +678,12 @@
     hbm = pl.BlockSpec(memory_space=pl.ANY)
     n_p, n_z = 2 * n_y, n_x // 2
     field = pltpu.VMEM((POINTS, LANES), F32)
-    return pl.pallas_call(
+    whole = jax.ShapeDtypeStruct((POINTS, LANES), F32)
+    direction, image, sums = pl.pallas_call(
         functools.partial(kernel, n_x, n_y),
-        out_shape=(
-            jax.ShapeDtypeStruct((POINTS, LANES), F32),
-            jax.ShapeDtypeStruct((POINTS, LANES), F32),
-            jax.ShapeDtypeStruct((1,), F32),
-        ),
-        in_specs=[hbm] * len(args),
-        out_specs=(hbm, hbm, smem),
+        out_shape=(whole, whole, jax.ShapeDtypeStruct((1, LANES), F32)),
+        in_specs=[hbm] * 12,
+        out_specs=(hbm, hbm, hbm),
         scratch_shapes=[
             pltpu.SMEM((1,), jnp.int32),
             pltpu.VMEM(vid.shape, jnp.int32),
@@ -616,7 +692,6 @@
             pltpu.VMEM(scode.shape, jnp.int32),
             pltpu.VMEM(pface.shape, jnp.int32),
             pltpu.VMEM(pcode.shape, jnp.int32),
-            field,
             field,
             pltpu.VMEM((3, POINTS, LANES), BF16),
             pltpu.VMEM((3, POINTS, LANES), BF16),
@@ -657,15 +732,35 @@
             pltpu.VMEM((n_p, 1, LANES), F32),
             pltpu.VMEM((1, LANES), F32),
             pltpu.VMEM((n_z, 1, LANES), F32),
+            pltpu.VMEM((1, LANES), F32),
+            pltpu.SemaphoreType.REGULAR,
             pltpu.SemaphoreType.DMA((13,)),
-            pltpu.SemaphoreType.DMA((2, 2)),
+            pltpu.SemaphoreType.DMA((3,)),
             pltpu.SemaphoreType.DMA((10,)),
             pltpu.SemaphoreType.DMA((10,)),
         ],
         compiler_params=pltpu.CompilerParams(
             collective_id=0, has_side_effects=True, vmem_limit_bytes=60 * 1024 * 1024
         ),
-    )(*args)
+    )(*args[1:])
+    return pl.pallas_call(
+        update,
+        out_shape=(whole, whole, jax.ShapeDtypeStruct((1,), F32)),
+        in_specs=[hbm] * 6,
+        out_specs=(hbm, hbm, smem),
+        scratch_shapes=[
+            field,
+            field,
+            field,
+            field,
+            pltpu.VMEM((1, LANES), F32),
+            pltpu.SMEM((1,), jnp.int32),
+            pltpu.SemaphoreType.DMA((2, 4)),
+            pltpu.SemaphoreType.DMA((2,)),
+            pltpu.SemaphoreType.DMA((2, 2)),
+        ],
+        compiler_params=pltpu.CompilerParams(vmem_limit_bytes=60 * 1024 * 1024),
+    )(args[0], args[1], direction, image, sums, live)
 
 
 def solution(mesh):

time: 66.6 us -> 62.6 us (0.940)
  local copies, waits for them, and re-layouts: 2.42 us -> 0 us
  between operations: 3.06 us -> 1.29 us
    unnamed x4 -> x0, local copies, waits for them, and re-layouts: 2.42 us -> none
    pallas_call x1 -> x2, Pallas kernels: 61 us -> 61.1 us  [the longest x1 58.5 us: on_device(): pl.pallas_call(functools.partial(kernel, n_x, n_y), out_shape=(whole, who...]
where the time goes in v3:
time: 62.6 us; the launch traced here: 62.4 us
  Pallas kernels  61.1 us (98%)
  between operations  1.29 us (2%)
    pallas_call x1, Pallas kernels, on_device(): pl.pallas_call(functools.partial(kernel, n_x, n_y), out_shape=(whole, who...  58.5 us
    pallas_call x1, Pallas kernels, on_device(): pl.pallas_call(update, out_shape=(whole, whole, jax.ShapeDtypeStruct((1,)...  2.65 us

profile of v3, /device:TPU:1, one launch (start us, length us, event | category | flops | bytes accessed | tf_op | source)
XLA Modules:
  0.0 62.4 jit_solution(12298067437979825463)
XLA Ops:
  1.3 58.5 %shard_map.148 = (f32[512,128]{1,0:T(8,128)}, f32[512,128]{1,0:T(8,128)}, f32[1,128]{1,0:T(1,128)}) custom-call(f32[512,128]{1,0:T(8,128)} %res_hbm.3, bf16[3,512,128]{2,1,0:T(8,128)(2,1)} %diag_hbm.1, bf16[3,512,128]{2,1,0:T(8,128)(2,1)} %cross_hbm.1, f32[3,8,8,128]{3,2,1,0:T(8,128)} %fdm_hbm.1, f32[3,8,128]{2,1,0:T(8,128)} %eig_hbm.1, s32[8,128]{1,0:T(8,128)} %vid_hbm.1, ...), custom_call_target="tpu_custom_call" | custom-call | tf_op jit(solution)/shard_map/pallas_call | solution.py:682
  59.8 2.6 %shard_map.149 = (f32[512,128]{1,0:T(8,128)}, f32[512,128]{1,0:T(8,128)}, f32[1]{0:T(128)}) custom-call(f32[512,128]{1,0:T(8,128)} %sol_hbm.1, f32[512,128]{1,0:T(8,128)} %res_hbm.3, f32[512,128]{1,0:T(8,128)} %get-tuple-element.6.direction_hbm, f32[512,128]{1,0:T(8,128)} %get-tuple-element.7.image_hbm, f32[1,128]{1,0:T(1,128)} %get-tuple-element.8.sums_hbm, ...), custom_call_target="tpu_custom_call" | custom-call | tf_op jit(solution)/shard_map/pallas_call | solution.py:746

commit v4 on v3

--- a/solution.py
+++ b/solution.py
@@ -81,6 +81,7 @@
 def kernel(
     n_x,
     n_y,
+    sol_hbm,
     res_hbm,
     diag_hbm,
     cross_hbm,
@@ -93,9 +94,11 @@
     scode_hbm,
     pface_hbm,
     pcode_hbm,
-    direction_out,
-    image_out,
-    sums_out,
+    sol,
+    rm,
+    direction,
+    field,
+    totals,
     live_ref,
     vid_ref,
     eig_ref,
@@ -103,7 +106,6 @@
     scode_ref,
     pface_ref,
     pcode_ref,
-    rm,
     diag,
     cross,
     fdm,
@@ -111,11 +113,9 @@
     blocks,
     buf_a,
     buf_b,
-    field,
     turned,
     turned2,
     grad1,
-    direction,
     x_one,
     y_one,
     h_one,
@@ -143,10 +143,8 @@
     rc_a,
     own_b,
     rc_b,
-    totals,
     ready,
     in_sem,
-    out_sem,
     send_sem,
     recv_sem,
 ):
@@ -169,6 +167,7 @@
         eig=(eig_hbm, eig_ref),
         diag=(diag_hbm, diag),
         cross=(cross_hbm, cross),
+        sol=(sol_hbm, sol),
     )
     loads = {n: pltpu.make_async_copy(s, d, in_sem.at[i]) for i, (n, (s, d)) in enumerate(moved.items())}
     for load in loads.values():
@@ -294,7 +293,7 @@
     send_plane(lambda t: part.at[t], rc1, 0)
     rc1[me] = part[me]
     send_plane(lambda t: inv_hbm.at[:, pl.ds(pl.multiple_of(256 * t, 256), 256)], block, 9)
-    keep = pltpu.make_async_copy(inv_hbm.at[:, pl.ds(pl.multiple_of(256 * me, 256), 256)], block.at[me], in_sem.at[12])
+    keep = pltpu.make_async_copy(inv_hbm.at[:, pl.ds(pl.multiple_of(256 * me, 256), 256)], block.at[me], in_sem.at[13])
     keep.start()
 
     def column(row, rows, swap=0):
@@ -516,9 +515,6 @@
         lifted = float(HATS[0, i]) * planes[0] + float(HATS[1, i]) * planes[1]
         direction[at, :] = alive * (field[at, :] + lifted)
 
-    stores = [pltpu.make_async_copy(direction, direction_out, out_sem.at[0])]
-    stores[0].start()
-
     def take(ref, start, stride):
         return [ref[pl.ds(pl.multiple_of(start + stride * m, 8), 8), :] for m in range(EDGE)]
 
@@ -580,11 +576,11 @@
         return jnp.sum((a * b).reshape(POINTS // EDGE, EDGE, LANES), axis=0)
 
     old = folded(rm[...], rm[...])
+    loads["sol"].wait()
+    sol[...] = sol[...] * alive
     await_faces(8, inc2)
     place_faces(field, inc2)
 
-    stores.append(pltpu.make_async_copy(field, image_out, out_sem.at[1]))
-    stores[1].start()
     image = field[...]
     mixed = folded(rm[...], image)
     square = folded(image, image)
@@ -604,49 +600,11 @@
     sums = jnp.sum(rc_b[...], axis=0)
 
     totals[...] = sums
-    stores.append(pltpu.make_async_copy(totals, sums_out, out_sem.at[2]))
-    stores[2].start()
     for phase, some in sent:
         pltpu.make_async_copy(some, some, send_sem.at[phase]).wait()
-    for store in stores:
-        store.wait()
-
-
-def update(
-    sol_hbm,
-    res_hbm,
-    direction_hbm,
-    image_hbm,
-    sums_hbm,
-    live_hbm,
-    sol_out,
-    res_out,
-    ratio_out,
-    sol,
-    res,
-    direction,
-    image,
-    sums_ref,
-    live_ref,
-    in_sem,
-    small_sem,
-    out_sem,
-):
-    small = [
-        pltpu.make_async_copy(s, d, small_sem.at[i]) for i, (s, d) in enumerate(((sums_hbm, sums_ref), (live_hbm, live_ref)))
-    ]
-    for copy in small:
-        copy.start()
-    half = POINTS // 2
-    loads = []
-    for h in range(2):
-        at = pl.ds(half * h, half)
-        for q, (s, d) in enumerate(((sol_hbm, sol), (direction_hbm, direction), (res_hbm, res), (image_hbm, image))):
-            loads.append(pltpu.make_async_copy(s.at[at], d.at[at], in_sem.at[h, q]))
-    for copy in loads:
-        copy.start()
-    for copy in small:
-        copy.wait()
+
+
+def update(sol, res, direction, image, sums_ref, sol_out, res_out, ratio_out, moved, left, sem):
     lane = iota((1, LANES), 1)
     sums = sums_ref[...]
 
@@ -654,16 +612,16 @@
         return jnp.sum(jnp.where(lane == q, sums, 0.0), axis=1, keepdims=True)
 
     step = total(0) / total(1)
-    alive = (lane < live_ref[0]).astype(F32)
+    parts = 4
+    rows = POINTS // parts
     stores = []
-    for h in range(2):
-        at = pl.ds(half * h, half)
-        for copy in loads[4 * h : 4 * h + 4]:
-            copy.wait()
-        sol[at, :] = alive * (sol[at, :] + step * direction[at, :])
-        res[at, :] = res[at, :] * alive - step * image[at, :]
-        for q, (s, d) in enumerate(((sol, sol_out), (res, res_out))):
-            store = pltpu.make_async_copy(s.at[at], d.at[at], out_sem.at[h, q])
+    for h in range(parts):
+        at = pl.ds(rows * h, rows)
+        for q, (ref, value, out) in enumerate(
+            ((moved, sol[at, :] + step * direction[at, :], sol_out), (left, res[at, :] - step * image[at, :], res_out))
+        ):
+            ref[at, :] = value
+            store = pltpu.make_async_copy(ref.at[at], out.at[at], sem.at[h, q])
             store.start()
             stores.append(store)
     ratio = (total(2) - 2.0 * step * total(3) + step * step * total(4)) / total(2)
@@ -675,15 +633,17 @@
 def on_device(n_x, n_y, *args):
     live, vid, eig, sface, scode, pface, pcode = (args[i] for i in (8, 6, 5, 9, 10, 11, 12))
     smem = pl.BlockSpec(memory_space=pltpu.SMEM)
+    vmem = pl.BlockSpec(memory_space=pltpu.VMEM)
     hbm = pl.BlockSpec(memory_space=pl.ANY)
     n_p, n_z = 2 * n_y, n_x // 2
     field = pltpu.VMEM((POINTS, LANES), F32)
     whole = jax.ShapeDtypeStruct((POINTS, LANES), F32)
-    direction, image, sums = pl.pallas_call(
+    held = [field] * 4 + [pltpu.VMEM((1, LANES), F32)]
+    results = pl.pallas_call(
         functools.partial(kernel, n_x, n_y),
-        out_shape=(whole, whole, jax.ShapeDtypeStruct((1, LANES), F32)),
-        in_specs=[hbm] * 12,
-        out_specs=(hbm, hbm, hbm),
+        out_shape=held,
+        in_specs=[hbm] * 13,
+        out_specs=[vmem] * 5,
         scratch_shapes=[
             pltpu.SMEM((1,), jnp.int32),
             pltpu.VMEM(vid.shape, jnp.int32),
@@ -692,14 +652,11 @@
             pltpu.VMEM(scode.shape, jnp.int32),
             pltpu.VMEM(pface.shape, jnp.int32),
             pltpu.VMEM(pcode.shape, jnp.int32),
-            field,
             pltpu.VMEM((3, POINTS, LANES), BF16),
             pltpu.VMEM((3, POINTS, LANES), BF16),
             pltpu.VMEM((3, EDGE, EDGE, LANES), F32),
             pltpu.VMEM((n_p, 16, 2 * LANES), F32),
             pltpu.VMEM((32 * n_p, 2 * LANES), BF16),
-            field,
-            field,
             field,
             field,
             field,
@@ -732,35 +689,23 @@
             pltpu.VMEM((n_p, 1, LANES), F32),
             pltpu.VMEM((1, LANES), F32),
             pltpu.VMEM((n_z, 1, LANES), F32),
-            pltpu.VMEM((1, LANES), F32),
             pltpu.SemaphoreType.REGULAR,
-            pltpu.SemaphoreType.DMA((13,)),
-            pltpu.SemaphoreType.DMA((3,)),
+            pltpu.SemaphoreType.DMA((14,)),
             pltpu.SemaphoreType.DMA((10,)),
             pltpu.SemaphoreType.DMA((10,)),
         ],
         compiler_params=pltpu.CompilerParams(
             collective_id=0, has_side_effects=True, vmem_limit_bytes=60 * 1024 * 1024
         ),
-    )(*args[1:])
+    )(*args)
     return pl.pallas_call(
         update,
         out_shape=(whole, whole, jax.ShapeDtypeStruct((1,), F32)),
-        in_specs=[hbm] * 6,
+        in_specs=[vmem] * 5,
         out_specs=(hbm, hbm, smem),
-        scratch_shapes=[
-            field,
-            field,
-            field,
-            field,
-            pltpu.VMEM((1, LANES), F32),
-            pltpu.SMEM((1,), jnp.int32),
-            pltpu.SemaphoreType.DMA((2, 4)),
-            pltpu.SemaphoreType.DMA((2,)),
-            pltpu.SemaphoreType.DMA((2, 2)),
-        ],
+        scratch_shapes=[field, field, pltpu.SemaphoreType.DMA((4, 2))],
         compiler_params=pltpu.CompilerParams(vmem_limit_bytes=60 * 1024 * 1024),
-    )(args[0], args[1], direction, image, sums, live)
+    )(*[pltpu.with_memory_space_constraint(r, pltpu.VMEM) for r in results])
 
 
 def solution(mesh):

time: 62.6 us -> 60.9 us (0.973)
  Pallas kernels: 61.1 us -> 59.4 us
    pallas_call x1, Pallas kernels: 2.65 us -> 1.46 us  [on_device(): pl.pallas_call(update, out_shape=(whole, whole, jax.ShapeDtypeStruct((1,)...]
where the time goes in v4:
time: 60.9 us; the launch traced here: 60.7 us
  Pallas kernels  59.4 us (98%)
  between operations  1.29 us (2%)
    pallas_call x1, Pallas kernels, on_device(): pl.pallas_call(functools.partial(kernel, n_x, n_y), out_shape=held, in_sp...  58 us
    pallas_call x1, Pallas kernels, on_device(): pl.pallas_call(update, out_shape=(whole, whole, jax.ShapeDtypeStruct((1,)...  1.46 us

profile of v4, /device:TPU:1, one launch (start us, length us, event | category | flops | bytes accessed | tf_op | source)
XLA Modules:
  0.0 60.7 jit_solution(634765303610191291)
XLA Ops:
  1.3 58.0 %shard_map.148 = (f32[512,128]{1,0:T(8,128)S(1)}, f32[512,128]{1,0:T(8,128)S(1)}, f32[512,128]{1,0:T(8,128)S(1)}, f32[512,128]{1,0:T(8,128)S(1)}, f32[1,128]{1,0:T(1,128)S(1)}) custom-call(f32[512,128]{1,0:T(8,128)} %sol_hbm.1, f32[512,128]{1,0:T(8,128)} %res_hbm.1, bf16[3,512,128]{2,1,0:T(8,128)(2,1)} %diag_hbm.1, bf16[3,512,128]{2,1,0:T(8,128)(2,1)} %cross_hbm.1, ...), custom_call_target="tpu_custom_call" | custom-call | tf_op jit(solution)/shard_map/pallas_call | solution.py:642
  59.3 1.5 %shard_map.149 = (f32[512,128]{1,0:T(8,128)}, f32[512,128]{1,0:T(8,128)}, f32[1]{0:T(128)}) custom-call(f32[512,128]{1,0:T(8,128)S(1)} %get-tuple-element.8.sol, f32[512,128]{1,0:T(8,128)S(1)} %get-tuple-element.9.res, f32[512,128]{1,0:T(8,128)S(1)} %get-tuple-element.10.direction, f32[512,128]{1,0:T(8,128)S(1)} %get-tuple-element.11.image, ...), custom_call_target="tpu_custom_call" | custom-call | tf_op jit(solution)/shard_map/pallas_call | solution.py:701

commit v5 on v4

--- a/solution.py
+++ b/solution.py
@@ -170,9 +170,6 @@
         sol=(sol_hbm, sol),
     )
     loads = {n: pltpu.make_async_copy(s, d, in_sem.at[i]) for i, (n, (s, d)) in enumerate(moved.items())}
-    for load in loads.values():
-        load.start()
-
     barrier = pltpu.get_barrier_semaphore()
 
     def at_plane(k):
@@ -210,6 +207,9 @@
     @pl.when(core == 1)
     def _():
         pl.semaphore_signal(barrier, inc=1, **at_device(2 * z, y))
+
+    for load in loads.values():
+        load.start()
 
     over_line(lambda t: pl.semaphore_signal(barrier, inc=1, **at_device(2 * t + 1, y)))
 
@@ -422,9 +422,6 @@
         out[...] = found
         inc[pl.ds(FIRST, 32), :] = found[0:32]
         hops = [
-            (PEER_ROW + PEER_ROWS * g, PEER_ROW + PEER_ROWS * back_to[g], PEER_ROWS, (x, lax.rem(y + offsets[g], n_y)))
-            for g in range(5)
-        ] + [
             (
                 PIPE_ROW + PIPE_ROWS * s,
                 PIPE_ROW + PIPE_ROWS * (1 - s),
@@ -432,6 +429,14 @@
                 (lax.rem(x + n_x - 1 + 2 * s, n_x), y),
             )
             for s in range(2)
+        ] + [
+            (
+                PEER_ROW + PEER_ROWS * g,
+                PEER_ROW + PEER_ROWS * back_to[g],
+                PEER_ROWS,
+                (x, lax.rem(y + offsets[g], n_y)),
+            )
+            for g in range(5)
         ]
         for start, land, count, target in hops:
             send(out.at[pl.ds(start, count)], inc.at[pl.ds(land, count)], phase, *target)
@@ -516,15 +521,16 @@
         direction[at, :] = alive * (field[at, :] + lifted)
 
     def take(ref, start, stride):
-        return [ref[pl.ds(pl.multiple_of(start + stride * m, 8), 8), :] for m in range(EDGE)]
+        return [ref[pl.ds(start + stride * m, 8), :] for m in range(EDGE)]
 
     def along_first(j, c):
         result = mirrored(D_EVEN, D_ODD, take(direction, 8 * j, 64))
         for a in range(EDGE):
-            grad1[pl.ds(pl.multiple_of(64 * a + 8 * j, 8), 8), :] = result[a]
+            grad1[pl.ds(64 * a + 8 * j, 8), :] = result[a]
         return c
 
-    lax.fori_loop(0, EDGE, along_first, 0)
+    for j in range(EDGE):
+        along_first(j, 0)
 
     def turn(values, ref):
         for m in range(EDGE):
@@ -533,11 +539,11 @@
 
     def middle(i, sums):
         curve, dots = sums
-        start = pl.multiple_of(64 * i, 64)
+        start = 64 * i
         slab = pl.ds(start, 64)
         d = take(direction, start, 8)
-        across = turn(d, turned.at[pl.ds(0, 64)])
-        g3 = turn(mirrored(D_EVEN, D_ODD, across), turned.at[pl.ds(64, 64)])
+        across = turn(d, turned.at[slab])
+        g3 = turn(mirrored(D_EVEN, D_ODD, across), turned2.at[slab])
         g2 = mirrored(D_EVEN, D_ODD, d)
         g1 = take(grad1, start, 8)
         m = [diag[q, slab, :].astype(F32) for q in range(3)] + [cross[q, slab, :].astype(F32) for q in range(3)]
@@ -552,23 +558,27 @@
             f2.append(v)
             f3.append(w)
         dots = dots + jnp.sum((rm[slab, :] * direction[slab, :]).reshape(EDGE, EDGE, LANES), axis=0)
-        b3 = turn(mirrored(T_EVEN, T_ODD, turn(f3, turned2.at[pl.ds(0, 64)])), turned2.at[pl.ds(64, 64)])
+        b3 = turn(mirrored(T_EVEN, T_ODD, turn(f3, buf_a.at[slab])), buf_b.at[slab])
         b2 = mirrored(T_EVEN, T_ODD, f2)
         for j in range(EDGE):
             field[pl.ds(start + 8 * j, 8), :] = (b2[j] + b3[j]) + d[j]
         return curve, dots
 
     zero = jnp.zeros((EDGE, LANES), F32)
-    curve, dots = lax.fori_loop(0, EDGE, middle, (zero, zero))
+    sums = (zero, zero)
+    for i in range(EDGE):
+        sums = middle(i, sums)
+    curve, dots = sums
 
     def back_first(j, c):
         result = mirrored(T_EVEN, T_ODD, take(grad1, 8 * j, 64))
         for a in range(EDGE):
-            at = pl.ds(pl.multiple_of(64 * a + 8 * j, 8), 8)
+            at = pl.ds(64 * a + 8 * j, 8)
             field[at, :] = field[at, :] + result[a]
         return c
 
-    lax.fori_loop(0, EDGE, back_first, 0)
+    for j in range(EDGE):
+        back_first(j, 0)
 
     send_faces(field, out2, inc2, 8)
 

time: 60.9 us -> 60.6 us (level)
  no operation moved by 1% of the time
where the time goes in v5:
time: 60.6 us; the launch traced here: 60.4 us
  Pallas kernels  59.1 us (98%)
  between operations  1.29 us (2%)
    pallas_call x1, Pallas kernels, on_device(): pl.pallas_call(functools.partial(kernel, n_x, n_y), out_shape=held, in_sp...  57.7 us
    pallas_call x1, Pallas kernels, on_device(): pl.pallas_call(update, out_shape=(whole, whole, jax.ShapeDtypeStruct((1,)...  1.46 us

profile of v5, /device:TPU:1, one launch (start us, length us, event | category | flops | bytes accessed | tf_op | source)
XLA Modules:
  0.0 60.4 jit_solution(4205370430754614859)
XLA Ops:
  1.3 57.7 %shard_map.148 = (f32[512,128]{1,0:T(8,128)S(1)}, f32[512,128]{1,0:T(8,128)S(1)}, f32[512,128]{1,0:T(8,128)S(1)}, f32[512,128]{1,0:T(8,128)S(1)}, f32[1,128]{1,0:T(1,128)S(1)}) custom-call(f32[512,128]{1,0:T(8,128)} %sol_hbm.1, f32[512,128]{1,0:T(8,128)} %res_hbm.1, bf16[3,512,128]{2,1,0:T(8,128)(2,1)} %diag_hbm.1, bf16[3,512,128]{2,1,0:T(8,128)(2,1)} %cross_hbm.1, ...), custom_call_target="tpu_custom_call" | custom-call | tf_op jit(solution)/shard_map/pallas_call | solution.py:652
  59.0 1.5 %shard_map.149 = (f32[512,128]{1,0:T(8,128)}, f32[512,128]{1,0:T(8,128)}, f32[1]{0:T(128)}) custom-call(f32[512,128]{1,0:T(8,128)S(1)} %get-tuple-element.8.sol, f32[512,128]{1,0:T(8,128)S(1)} %get-tuple-element.9.res, f32[512,128]{1,0:T(8,128)S(1)} %get-tuple-element.10.direction, f32[512,128]{1,0:T(8,128)S(1)} %get-tuple-element.11.image, ...), custom_call_target="tpu_custom_call" | custom-call | tf_op jit(solution)/shard_map/pallas_call | solution.py:711

commit v6 on v4

--- a/solution.py
+++ b/solution.py
@@ -336,15 +336,15 @@
         fits = (source == (grid_lane & 63)) & ((grid_row < 64) if t < 4 else (grid_row >= 64))
         perm[:, pl.ds(t * LANES, LANES)] = fits.astype(F32).astype(BF16)
 
+    @pl.when(core == 1)
+    def _():
+        pl.semaphore_wait(barrier, 2 * (n_z - 1))
+        pl.semaphore_signal(ready, inc=1, **at_device(2 * z, y))
+
     await_all(0, rc1, n_p)
     mine = jnp.sum(rc1[...], axis=0)
     own2[...] = mine
     rc2[z] = mine
-
-    @pl.when(core == 1)
-    def _():
-        pl.semaphore_wait(barrier, 2 * (n_z - 1))
-        pl.semaphore_signal(ready, inc=1, **at_device(2 * z, y))
 
     @pl.when(core == 0)
     def _():

time: 60.9 us -> 60.9 us (level)
  no operation moved by 1% of the time
where the time goes in v6:
time: 60.9 us; the launch traced here: 60.7 us
  Pallas kernels  59.4 us (98%)
  between operations  1.29 us (2%)
    pallas_call x1, Pallas kernels, on_device(): pl.pallas_call(functools.partial(kernel, n_x, n_y), out_shape=held, in_sp...  58 us
    pallas_call x1, Pallas kernels, on_device(): pl.pallas_call(update, out_shape=(whole, whole, jax.ShapeDtypeStruct((1,)...  1.46 us

profile of v6, /device:TPU:1, one launch (start us, length us, event | category | flops | bytes accessed | tf_op | source)
XLA Modules:
  0.0 60.7 jit_solution(919205058462595150)
XLA Ops:
  1.3 58.0 %shard_map.148 = (f32[512,128]{1,0:T(8,128)S(1)}, f32[512,128]{1,0:T(8,128)S(1)}, f32[512,128]{1,0:T(8,128)S(1)}, f32[512,128]{1,0:T(8,128)S(1)}, f32[1,128]{1,0:T(1,128)S(1)}) custom-call(f32[512,128]{1,0:T(8,128)} %sol_hbm.1, f32[512,128]{1,0:T(8,128)} %res_hbm.1, bf16[3,512,128]{2,1,0:T(8,128)(2,1)} %diag_hbm.1, bf16[3,512,128]{2,1,0:T(8,128)(2,1)} %cross_hbm.1, ...), custom_call_target="tpu_custom_call" | custom-call | tf_op jit(solution)/shard_map/pallas_call | solution.py:642
  59.2 1.5 %shard_map.149 = (f32[512,128]{1,0:T(8,128)}, f32[512,128]{1,0:T(8,128)}, f32[1]{0:T(128)}) custom-call(f32[512,128]{1,0:T(8,128)S(1)} %get-tuple-element.8.sol, f32[512,128]{1,0:T(8,128)S(1)} %get-tuple-element.9.res, f32[512,128]{1,0:T(8,128)S(1)} %get-tuple-element.10.direction, f32[512,128]{1,0:T(8,128)S(1)} %get-tuple-element.11.image, ...), custom_call_target="tpu_custom_call" | custom-call | tf_op jit(solution)/shard_map/pallas_call | solution.py:701
